TPU v7x, 32 devices: a whole 2x2x4 slice. The times are simulated.
32 devices in a mesh: pair: 2 (over core), edge: 16 (over z, y, x).
Axes of the slice: x: 2, y: 2, z: 4, core: 2. Of those that a mesh axis runs over, the one named last changes fastest.
Arguments:
- edge_embed: float32 [32768, 512], P('edge', 'pair'), may hold values from -6 to 6
- atom_embed: float32 [1024, 256], P('edge', 'pair'), may hold values from -6 to 6
- edge_rbf: float32 [32768, 128], P('edge'), may hold values from 0 to 1
- edge_src: int32 [32768], P('edge'), may hold values from 0 to 191
- edge_dst: int32 [32768], P('edge'), may hold values from 0 to 63
- halo_send: int32 [2048], P('edge'), may hold values from 0 to 63
- trip_index: int32 [32768, 16], P('edge'), may hold values from 0 to 2047
- trip_cos: float32 [32768, 16], P('edge'), may hold values from -1 to 1
- trip_live: int32 [32768, 16], P('edge'), may hold values 0 or 1
- quad_index: int32 [8192, 8], P('edge'), may hold values from 0 to 2047
- quad_cos: float32 [8192, 8], P('edge'), may hold values from -1 to 1
- quad_dih: float32 [8192, 8], P('edge'), may hold values from -1 to 1
- quad_live: int32 [8192, 8], P('edge'), may hold values 0 or 1
- quad_target: int32 [8192], P('edge'), may hold values from 0 to 2047
- w_quad_rbf: float32 [128, 512], replicated, may hold values from -0.5 to 0.5
- w_quad_down: float32 [512, 32], replicated, may hold values from -0.25 to 0.25
- w_quad_bil: float32 [1024, 32], replicated, may hold values from -0.375 to 0.375
- w_quad_up: float32 [32, 512], replicated, may hold values from -1 to 1
- w_trip_rbf: float32 [128, 512], replicated, may hold values from -0.5 to 0.5
- w_trip_down: float32 [512, 64], replicated, may hold values from -0.25 to 0.25
- triplet_bilinear_weight: float32 [1024, 64], replicated, may hold values from -0.375 to 0.375
- w_trip_up: float32 [64, 512], replicated, may hold values from -0.75 to 0.75
- w_res_one: float32 [512, 512], replicated, may hold values from -0.25 to 0.25
- w_res_two: float32 [512, 512], replicated, may hold values from -0.5 to 0.5
- w_atom_edge: float32 [1024, 512], replicated, may hold values from -0.1875 to 0.1875
- w_edge_rbf: float32 [128, 512], replicated, may hold values from -0.5 to 0.5
- w_edge_atom: float32 [512, 256], replicated, may hold values from -0.5 to 0.5
- w_out: float32 [256, 256], replicated, may hold values from -0.375 to 0.375
- cot_edge: float32 [32768, 512], P('edge', 'pair'), may hold values from -6 to 6
- cot_atom: float32 [1024, 256], P('edge', 'pair'), may hold values from -6 to 6
- cot_feat: float32 [1024, 256], P('edge', 'pair'), may hold values from -6 to 6
Outputs:
- edge_out: float32 [32768, 512], P('edge', 'pair')
- atom_out: float32 [1024, 256], P('edge', 'pair')
- atom_feat: float32 [1024, 256], P('edge', 'pair')
- grad_edge: float32 [32768, 512], P('edge', 'pair')
- grad_atom: float32 [1024, 256], P('edge', 'pair')
- grad_quad_rbf: float32 [128, 512], replicated
- grad_quad_down: float32 [512, 32], replicated
- grad_quad_bil: float32 [1024, 32], replicated
- grad_quad_up: float32 [32, 512], replicated
- grad_trip_rbf: float32 [128, 512], replicated
- grad_trip_down: float32 [512, 64], replicated
- grad_trip_bil: float32 [1024, 64], replicated
- grad_trip_up: float32 [64, 512], replicated
- grad_res_one: float32 [512, 512], replicated
- grad_res_two: float32 [512, 512], replicated
- grad_atom_edge: float32 [1024, 512], replicated
- grad_edge_rbf: float32 [128, 512], replicated
- grad_edge_atom: float32 [512, 256], replicated
- grad_out: float32 [256, 256], replicated
Inputs may be any that keep to these rules, and one draw needn't show every extreme that they name: `edge_src`: A value below 64 is an atom row of the edge's own partition; a value v at or above it is received row v - 64 of step pool. `halo_send`: entry d * 8 + c of a partition's block is the atom row it sends to partition d as its c-th row. `trip_index`: rows within the edge's own partition. `quad_index`: rows within the quadruplet row's own partition; quadruplet rows d * 32 to d * 32 + 31 of a partition go to partition d. `quad_target`: entry s * 32 + c of a partition's block names the edge of that partition that row c sent by partition s adds to.
All inputs are finite; a program needn't handle non-finite values. No bound on the sum of `trip_live` or of `quad_live` on one device may be relied on, other than what follows from the above.
Results may differ from a plain program's by a relative error of at most 0.0003.
Values sent between devices are 32-bit elements; how exact they have to be, the bound alone decides.
No kernel may reach another device: no remote copies, remote signals or barrier semaphores. Data moves between devices by JAX's collectives and lax.ppermute only.
A program may use at most 256 MiB of HBM per device.

v0:
```python
import jax
import jax.numpy as jnp
from jax import lax
from jax.sharding import PartitionSpec as P

root_third = 0.5773502691896258
root_half = 0.7071067811865476


def shifted(shard, axis, by):
    peers = lax.axis_size(axis)
    pairs = [(i, i + by) for i in range(peers) if 0 <= i + by < peers]
    return lax.ppermute(shard, axis, pairs)


def matmul(left, right):
    return jnp.dot(left, right, precision=lax.Precision.HIGHEST, preferred_element_type=jnp.float32)


def legendre(cosine, orders):
    series = [jnp.ones_like(cosine), cosine]
    for order in range(1, orders - 1):
        series.append(((2 * order + 1) * cosine * series[-1] - order * series[-2]) / (order + 1))
    return jnp.stack(series[:orders], axis=-1)


def triplet_expansion(cosine, live_slots, orders):
    return legendre(cosine, orders) * live_slots.astype(jnp.float32)[..., None]


def quadruplet_expansion(cosine, dihedral, live_slots, orders):
    angular = triplet_expansion(cosine, live_slots, orders)
    return jnp.concatenate([angular, angular * dihedral[..., None]], axis=-1)


def local_quad(embedding, radial, indices, basis_values, quad_weights):
    w_radial, w_down, w_bilinear = quad_weights
    mixed = jax.nn.silu(matmul(embedding * matmul(radial, w_radial), w_down))
    selected_rows = mixed[indices]
    basis_product = jnp.einsum(
        "pcd,pce->pde", basis_values, selected_rows, precision=lax.Precision.HIGHEST
    )
    return matmul(basis_product.reshape(basis_product.shape[0], -1), w_bilinear)


def local_interaction(
    embedding,
    atom_rows,
    halo_rows,
    quad_sum,
    radial,
    sources,
    targets,
    indices,
    basis_values,
    inter_weights,
):
    (
        w_radial,
        w_down,
        w_bilinear,
        w_lift,
        w_res_one,
        w_res_two,
        w_atom_edge,
        w_edge_rbf,
        w_edge_atom,
        w_out,
    ) = inter_weights
    mixed = jax.nn.silu(matmul(embedding * matmul(radial, w_radial), w_down))
    selected_rows = mixed[indices]
    basis_product = jnp.einsum(
        "eks,eki->esi", basis_values, selected_rows, precision=lax.Precision.HIGHEST
    )
    triplet = matmul(matmul(basis_product.reshape(basis_product.shape[0], -1), w_bilinear), w_lift)
    joined = (embedding + triplet + quad_sum) * root_third
    hidden = jax.nn.silu(matmul(joined, w_res_one))
    residual = (joined + jax.nn.silu(matmul(hidden, w_res_two))) * root_half
    atom_pool = jnp.concatenate([atom_rows, halo_rows], axis=0)
    stacked = jnp.concatenate([atom_pool[sources], atom_rows[targets], residual], axis=1)
    edge_new = (residual + jax.nn.silu(matmul(stacked, w_atom_edge))) * root_half
    weighted = edge_new * matmul(radial, w_edge_rbf)
    member = (targets[None, :] == jnp.arange(atom_rows.shape[0], dtype=jnp.int32)[:, None]).astype(
        jnp.float32
    )
    collected = matmul(member, weighted) * (atom_rows.shape[0] / embedding.shape[0]) ** 0.5
    atom_new = (atom_rows + jax.nn.silu(matmul(collected, w_edge_atom))) * root_half
    feature = jax.nn.silu(matmul(atom_new, w_out))
    return (edge_new, atom_new, feature)


def local(
    edge_embed,
    atom_embed,
    edge_rbf,
    edge_src,
    edge_dst,
    halo_send,
    trip_index,
    trip_cos,
    trip_live,
    quad_index,
    quad_cos,
    quad_dih,
    quad_live,
    quad_target,
    w_quad_rbf,
    w_quad_down,
    w_quad_bil,
    w_quad_up,
    w_trip_rbf,
    w_trip_down,
    triplet_bilinear_weight,
    w_trip_up,
    w_res_one,
    w_res_two,
    w_atom_edge,
    w_edge_rbf,
    w_edge_atom,
    w_out,
    cot_edge,
    cot_atom,
    cot_feat,
):
    partitions = lax.axis_size("edge")
    role = lax.axis_index("pair")
    embedding, atom_rows, grad_out_edge, grad_out_atom, grad_out_feat = (
        lax.all_gather(edge_embed, "pair", axis=1, tiled=True),
        lax.all_gather(atom_embed, "pair", axis=1, tiled=True),
        lax.all_gather(cot_edge, "pair", axis=1, tiled=True),
        lax.all_gather(cot_atom, "pair", axis=1, tiled=True),
        lax.all_gather(cot_feat, "pair", axis=1, tiled=True),
    )
    edge_count = embedding.shape[0]
    width = embedding.shape[1]
    atom_width = atom_rows.shape[1]
    quad_count = quad_index.shape[0]
    halo_count = halo_send.shape[0]
    orders = triplet_bilinear_weight.shape[0] // w_trip_down.shape[1]
    quad_weights = (w_quad_rbf, w_quad_down, w_quad_bil)
    inter_weights = (
        w_trip_rbf,
        w_trip_down,
        triplet_bilinear_weight,
        w_trip_up,
        w_res_one,
        w_res_two,
        w_atom_edge,
        w_edge_rbf,
        w_edge_atom,
        w_out,
    )

    def quad_forward(quad_embedding, weight_set, lift):
        basis_values = quadruplet_expansion(quad_cos, quad_dih, quad_live, orders)
        narrow_rows = local_quad(quad_embedding, edge_rbf, quad_index, basis_values, weight_set)
        return matmul(narrow_rows, lift)

    def interact(inter_embedding, inter_atoms, halo_rows, quad_part, weight_set, lift):
        basis_values = triplet_expansion(trip_cos, trip_live, orders)
        return local_interaction(
            inter_embedding,
            inter_atoms,
            halo_rows,
            quad_part,
            edge_rbf,
            edge_src,
            edge_dst,
            trip_index,
            basis_values,
            weight_set,
        )

    quad_send = lax.cond(
        role == 0,
        lambda: quad_forward(embedding, quad_weights, w_quad_up),
        lambda: jnp.zeros((quad_count, width), jnp.float32),
    )
    halo_out = atom_rows[halo_send].reshape(partitions, -1)
    halo_rows = lax.all_to_all(halo_out, "edge", split_axis=0, concat_axis=0, tiled=True).reshape(
        halo_count, atom_width
    )
    handed = shifted(quad_send.reshape(partitions, -1), "pair", 1)
    routed = lax.all_to_all(handed, "edge", split_axis=0, concat_axis=0, tiled=True).reshape(
        quad_count, width
    )
    quad_part = jnp.zeros((edge_count, width), jnp.float32).at[quad_target].add(routed)

    def inter_branch():
        outputs, pullback = jax.vjp(
            interact, embedding, atom_rows, halo_rows, quad_part, inter_weights, w_quad_up
        )
        return (outputs, pullback((grad_out_edge, grad_out_atom, grad_out_feat)))

    def inter_spare():
        outputs = (jnp.zeros_like(embedding), jnp.zeros_like(atom_rows), jnp.zeros_like(atom_rows))
        grads = (
            jnp.zeros_like(embedding),
            jnp.zeros_like(atom_rows),
            jnp.zeros_like(halo_rows),
            jnp.zeros_like(quad_part),
            jax.tree.map(jnp.zeros_like, inter_weights),
            jnp.zeros_like(w_quad_up),
        )
        return (outputs, grads)

    outputs, grads = lax.cond(role == 1, inter_branch, inter_spare)
    edge_new, atom_new, feature = outputs
    grad_embedding, grad_atoms, grad_halo, grad_quad_part, grad_inter, grad_lift_inter = grads
    returned = lax.all_to_all(
        grad_quad_part[quad_target].reshape(partitions, -1),
        "edge",
        split_axis=0,
        concat_axis=0,
        tiled=True,
    )
    quad_grad = shifted(returned, "pair", -1).reshape(quad_count, width)

    def quad_branch():
        unused, pullback = jax.vjp(quad_forward, embedding, quad_weights, w_quad_up)
        return pullback(quad_grad)

    def quad_spare():
        return (
            jnp.zeros_like(embedding),
            jax.tree.map(jnp.zeros_like, quad_weights),
            jnp.zeros_like(w_quad_up),
        )

    grad_embed_quad, grad_quad_weights, grad_lift_quad = lax.cond(
        role == 0, quad_branch, quad_spare
    )
    halo_grads = lax.all_to_all(
        grad_halo.reshape(partitions, -1), "edge", split_axis=0, concat_axis=0, tiled=True
    ).reshape(halo_count, atom_width)
    grad_atoms = grad_atoms + jnp.zeros_like(atom_rows).at[halo_send].add(halo_grads)
    summed = lax.psum(
        (
            grad_quad_weights[0],
            grad_quad_weights[1],
            grad_quad_weights[2],
            grad_lift_quad + grad_lift_inter,
            grad_inter[0],
            grad_inter[1],
            grad_inter[2],
            grad_inter[3],
            grad_inter[4],
            grad_inter[5],
            grad_inter[6],
            grad_inter[7],
            grad_inter[8],
            grad_inter[9],
        ),
        ("pair", "edge"),
    )
    halves_out = (
        lax.psum_scatter(edge_new, "pair", scatter_dimension=1, tiled=True),
        lax.psum_scatter(atom_new, "pair", scatter_dimension=1, tiled=True),
        lax.psum_scatter(feature, "pair", scatter_dimension=1, tiled=True),
        lax.psum_scatter(grad_embedding + grad_embed_quad, "pair", scatter_dimension=1, tiled=True),
        lax.psum_scatter(grad_atoms, "pair", scatter_dimension=1, tiled=True),
    )
    return (
        halves_out[0],
        halves_out[1],
        halves_out[2],
        halves_out[3],
        halves_out[4],
        summed[0],
        summed[1],
        summed[2],
        summed[3],
        summed[4],
        summed[5],
        summed[6],
        summed[7],
        summed[8],
        summed[9],
        summed[10],
        summed[11],
        summed[12],
        summed[13],
    )


def solution(mesh):
    in_specs = (
        P("edge", "pair"),
        P("edge", "pair"),
        P("edge", None),
        P("edge"),
        P("edge"),
        P("edge"),
        P("edge", None),
        P("edge", None),
        P("edge", None),
        P("edge", None),
        P("edge", None),
        P("edge", None),
        P("edge", None),
        P("edge"),
        P(),
        P(),
        P(),
        P(),
        P(),
        P(),
        P(),
        P(),
        P(),
        P(),
        P(),
        P(),
        P(),
        P(),
        P("edge", "pair"),
        P("edge", "pair"),
        P("edge", "pair"),
    )
    out_specs = (
        P("edge", "pair"),
        P("edge", "pair"),
        P("edge", "pair"),
        P("edge", "pair"),
        P("edge", "pair"),
        P(),
        P(),
        P(),
        P(),
        P(),
        P(),
        P(),
        P(),
        P(),
        P(),
        P(),
        P(),
        P(),
        P(),
    )
    return jax.shard_map(local, mesh=mesh, in_specs=in_specs, out_specs=out_specs, check_vma=False)
```

profile of v0, /device:TPU:0, one launch (start us, length us, event | category | flops | bytes accessed | tf_op | source)
XLA Modules:
  0.0 1175.6 jit_solution(2381985550937845017)
XLA Ops:
  8.8 17.3 %all-gather.3.cloned.1.call-done = f32[2048,512]{1,0:T(8,128)} async-done(((f32[2048,256]{1,0:T(8,128)}), f32[2048,512]{1,0:T(8,128)}) %all-gather.3.cloned.1.call-update) | async-done | bytes 4194320 | tf_op jit(solution)/shard_map/all_gather | solution.py:128
  26.1 53.5 %conditional.3 = (f32[512,512]{1,0:T(8,128)S(1)}) conditional(s32[]{:T(128)} %convert_element_type.18, () %tuple.42, (f32[512,8]{0,1:T(8,128)S(1)}, s32[512,8]{0,1:T(8,128)S(1)}, f32[512,8]{0,1:T(8,128)S(1)}, f32[2048,128]{1,0:T(8,128)S(1)}, f32[128,512]{1,0:T(8,128)}, /*index=5*/f32[2048,512]{1,0:T(8,128)}, f32[512,32]{0,1:T(8,128)S(1)}, ...), branch_computations={%region_0.0_spmd, %region_1.2_spmd} | conditional | flops 2367692800 | bytes 48889924 | solution.py:174
  33.1 4.0 divide_multiply_fusion
  37.5 14.7 %gather_fusion = f32[4096,32]{1,0:T(8,128)} fusion(f32[2048,32]{1,0:T(8,128)S(1)} %copy.1266, s32[4096]{0:T(1024)S(1)} %broadcast_clamp_fusion), kind=kCustom, calls=%fused_computation | custom fusion | bytes 1064960 | tf_op jit(solution)/shard_map/cond/branch_1_fun/gather | solution.py:39
  52.2 17.0 %fusion.2 = f32[512,32,32]{2,1,0:T(8,128)} fusion(f32[512,8,32]{2,1,0:T(8,128)} %copy.1267, f32[4096,32]{1,0:T(8,128)} %gather_fusion), kind=kOutput, calls=%fused_computation.15 | convolution fusion | flops 50331648 | bytes 3145728 | tf_op jit(solution)/shard_map/cond/branch_1_fun/pcd,pce->pde/dot_general | solution.py:40
  69.2 6.3 copy.1268
  85.6 6.8 all-to-all-start.1
  94.5 5.9 all-to-all-done.1
  100.4 3.7 all-to-all-start
  109.7 18.1 %all-to-all-done = f32[16,1,16384]{2,1,0:T(1,128)S(1)} async-done(((f32[16,1,16384]{2,1,0:T(1,128)}), f32[16,1,16384]{2,1,0:T(1,128)S(1)}, u32[]{:S(2)}, u32[]{:S(2)}) %all-to-all-start) | async-done | bytes 1048608 | tf_op jit(solution)/shard_map/all_to_all | solution.py:184
  130.6 5.9 scatter_custom_fusion.4
  136.5 19.9 %conditional.4 = (f32[2048,512]{1,0:T(8,128)}, f32[64,256]{1,0:T(8,128)S(1)}, f32[64,256]{1,0:T(8,128)S(1)}, f32[2048,512]{1,0:T(8,128)}, f32[64,256]{1,0:T(8,12...) conditional(s32[]{:T(128)} %convert_element_type.17, () %tuple.41, ...), branch_computations={%region_3.4_spmd.clone, %region_4.8_spmd.clone} | conditional | flops 96391872512 | bytes 807094336 | solution.py:207
  157.3 4.3 gather_fusion.6
  163.0 22.4 %all_to_all.41 = f32[16,1,16384]{2,1,0:T(1,128)S(1)} all-to-all(f32[16,1,16384]{2,1,0:T(1,128)S(1)} %all_to_all.36), channel_id=1, replica_groups=mesh['pair'=2,'edge'=16] {'edge'}, dimensions={0} | all-to-all | bytes 2097152 | tf_op jit(solution)/shard_map/all_to_all | solution.py:210
  189.1 3.9 all-to-all-start.3
  195.3 5.5 all-to-all-done.3
  203.8 617.8 %collective-permute-done.1 = f32[16,16384]{1,0:T(8,128)S(1)} collective-permute-done((f32[16,16384]{1,0:T(8,128)}, f32[16,16384]{1,0:T(8,128)S(1)}, u32[]{:S(2)}, u32[]{:S(2)}) %collective-permute-start.1) | collective-permute-done | bytes 1048608 | tf_op jit(solution)/shard_map/ppermute | solution.py:13
  821.7 122.5 %conditional.5 = (f32[2048,512]{1,0:T(8,128)}, f32[128,512]{0,1:T(8,128)}, f32[512,32]{0,1:T(8,128)}, f32[1024,32]{0,1:T(8,128)}, f32[32,512]{1,0:T(8,128)}) conditional(s32[]{:T(128)} %convert_element_type.18, () %tuple.45, (s32[512,8]{0,1:T(8,128)S(1)}, f32[512,8]{0,1:T(8,128)S(1)}, s32[512,8]{0,1:T(8,128)S(1)}, f32[512,8]{0,1:T(8,128)S(1)}, ...), branch_computations={%region_11.12_spmd, %region_12.14_spmd} | conditional | flops 5340667904 | bytes 107217760 | solution.py:230
  831.0 8.4 copy.1286
  839.4 9.9 convolution_bitcast_fusion
  849.3 23.1 %scatter_custom_fusion = f32[2048,32]{1,0:T(8,128)S(1)} fusion(s32[4096]{0:T(1024)S(1)} %reshape.157, f32[4096,32]{1,0:T(8,128)} %convolution_bitcast_fusion, f32[]{:T(128)} %constant.310.clone), kind=kCustom, calls=%fused_computation.60 | custom fusion | flops 131072 | bytes 262656 | tf_op jit(solution)/shard_map/cond/branch_1_fun/transpose(jvp())/scatter-add | solution.py:39
  872.7 6.7 fusion.104
  879.4 4.6 fusion.21
  888.6 14.2 %gather_fusion.1 = f32[4096,32]{1,0:T(8,128)} fusion(f32[2048,32]{1,0:T(8,128)S(1)} %copy.1289, s32[4096]{0:T(1024)S(1)} %broadcast_clamp_fusion.1), kind=kCustom, calls=%fused_computation.1 | custom fusion | bytes 1064960 | tf_op jit(solution)/shard_map/cond/branch_1_fun/jvp()/gather | solution.py:39
  902.8 7.1 fusion.105
  909.9 7.4 fusion.14
  917.4 16.1 %fusion.12 = f32[512,32,32]{2,1,0:T(8,128)} fusion(f32[512,8,32]{2,1,0:T(8,128)S(1)} %copy-done.11, f32[4096,32]{1,0:T(8,128)S(1)} %copy-done.18), kind=kOutput, calls=%fused_computation.55 | convolution fusion | flops 50331648 | bytes 3145728 | tf_op jit(solution)/shard_map/cond/branch_1_fun/jvp(pcd,pce->pde)/dot_general | solution.py:40
  933.5 5.2 copy.1291
  948.3 6.6 add.134
  955.1 162.6 %all-reduce.3.cloned.1.call-done = (f32[128,512]{1,0:T(8,128)}, f32[512,32]{0,1:T(8,128)}, f32[1024,32]{0,1:T(8,128)}, f32[32,512]{1,0:T(8,128)}, f32[128,512]{1...) async-done(((f32[128,512]{1,0:T(8,128)}, ...) | async-done | bytes 6553616 | tf_op jit(solution)/shard_map/psum | solution.py:237
  1117.7 15.2 %reduce-scatter.6.cloned.1.call-done = f32[2048,256]{1,0:T(8,128)} async-done(((f32[2048,512]{1,0:T(8,128)}), f32[2048,256]{1,0:T(8,128)}) %reduce-scatter.6.cloned.1.call-update) | async-done | bytes 2097168 | tf_op jit(solution)/shard_map/reduce_scatter | solution.py:257
  1132.8 16.2 %reduce-scatter.12.cloned.1.call-done = f32[2048,256]{1,0:T(8,128)} async-done(((f32[2048,512]{1,0:T(8,128)}), f32[2048,256]{1,0:T(8,128)}) %reduce-scatter.12.cloned.1.call-update) | async-done | bytes 2097168 | tf_op jit(solution)/shard_map/reduce_scatter | solution.py:260
  (254 shorter events, 97.9 us)
Async XLA Ops:
  7.3 18.8 %all-gather.3.cloned.1.call-start = ((), (), s32[]{:S(2)}) async-start(), calls=%async_computation.9 | async-start | bytes 6291456 | tf_op jit(solution)/shard_map/all_gather | solution.py:128
  8.0 128.5 %all-gather.5.cloned.1.call-start = ((), (), s32[]{:S(2)}) async-start(), calls=%async_computation.10 | async-start | bytes 6291456 | tf_op jit(solution)/shard_map/all_gather | solution.py:130
  26.1 55.1 %copy-start.86 = (f32[64,128]{1,0:T(8,128)S(1)}, f32[64,128]{1,0:T(8,128)}, u32[]{:S(2)}) copy-start(f32[64,128]{1,0:T(8,128)} %param.38) | copy-start | bytes 98308
  26.1 57.4 %copy-start.94 = (s32[128]{0:T(128)S(1)}, s32[128]{0:T(128)}, u32[]{:S(2)}) copy-start(s32[128]{0:T(128)} %param.42) | copy-start | bytes 1540
  79.6 26.5 %copy-start.88 = (f32[64,128]{1,0:T(8,128)S(1)}, f32[64,128]{1,0:T(8,128)}, u32[]{:S(2)}) copy-start(f32[64,128]{1,0:T(8,128)} %param.67) | copy-start | bytes 98308
  79.7 28.4 %copy-start.92 = (s32[512]{0:T(512)S(1)}, s32[512]{0:T(512)}, u32[]{:S(2)}) copy-start(s32[512]{0:T(512)} %param.50) | copy-start | bytes 6148
  79.9 12.6 %collective-permute-start = (f32[16,16384]{1,0:T(8,128)S(1)}, f32[16,16384]{1,0:T(8,128)S(1)}, u32[]{:S(2)}, u32[]{:S(2)}) collective-permute-start(f32[16,16384]{1,0:T(8,128)S(1)} %reshape.91), channel_id=1, source_target_pairs={{0,16},{1,17},{2,18},{3,19},{4,20},{5,21},{6,22},{7,23},{8,24},{9,... | collective-permute-start | bytes 3145736 | tf_op jit(solution)/shard_map/ppermute | solution.py:13
  85.6 14.8 %all-to-all-start.1 = ((f32[16,1,2048]{2,1,0:T(1,128)}), f32[16,1,2048]{2,1,0:T(1,128)S(1)}, u32[]{:S(2)}, u32[]{:S(2)}) async-start(f32[16,1,2048]{2,1,0:T(1,128)} %all_to_all.35), calls=%async_computation.1 | async-start | bytes 262144 | tf_op jit(solution)/shard_map/all_to_all | solution.py:180
  100.4 27.4 %all-to-all-start = ((f32[16,1,16384]{2,1,0:T(1,128)}), f32[16,1,16384]{2,1,0:T(1,128)S(1)}, u32[]{:S(2)}, u32[]{:S(2)}) async-start(f32[16,1,16384]{2,1,0:T(1,128)} %all_to_all.26), calls=%async_computation | async-start | bytes 2097152 | tf_op jit(solution)/shard_map/all_to_all | solution.py:184
  104.1 851.0 %reduce-scatter.10.cloned.1.call-start = ((), (), s32[]{:S(2)}) async-start(), calls=%async_computation.13 | async-start | bytes 98304 | tf_op jit(solution)/shard_map/reduce_scatter | solution.py:259
  109.7 26.8 %copy-start.31 = (f32[2048,16]{0,1:T(8,128)S(1)}, f32[2048,16]{0,1:T(8,128)}, u32[]{:S(2)}) copy-start(f32[2048,16]{0,1:T(8,128)} %param.44) | copy-start | bytes 393220
  109.7 26.8 %copy-start.54 = (f32[64,512]{1,0:T(8,128)S(1)}, f32[64,512]{1,0:T(8,128)}, u32[]{:S(2)}) copy-start(f32[64,512]{1,0:T(8,128)} %param.58) | copy-start | bytes 393220
  109.7 26.8 %copy-start.79 = (s32[2048]{0:T(1024)S(1)}, s32[2048]{0:T(1024)}, u32[]{:S(2)}) copy-start(s32[2048]{0:T(1024)} %param.41) | copy-start | bytes 24580
  109.7 26.8 %copy-start.89 = (s32[2048]{0:T(1024)S(1)}, s32[2048]{0:T(1024)}, u32[]{:S(2)}) copy-start(s32[2048]{0:T(1024)} %param.40) | copy-start | bytes 24580
  161.6 32.0 %copy-start.38 = (f32[128,512]{0,1:T(8,128)S(1)}, f32[128,512]{0,1:T(8,128)}, u32[]{:S(2)}) copy-start(f32[128,512]{0,1:T(8,128)} %get-tuple-element.214) | copy-start | bytes 786436
  161.7 39.5 %copy-start.91 = (s32[128]{0:T(128)S(1)}, s32[128]{0:T(128)}, u32[]{:S(2)}) copy-start(s32[128]{0:T(128)} %copy-done.90) | copy-start | bytes 1540
  162.9 31.5 %copy-start.40 = (f32[128,512]{0,1:T(8,128)S(1)}, f32[128,512]{0,1:T(8,128)}, u32[]{:S(2)}) copy-start(f32[128,512]{0,1:T(8,128)} %copy-done.39) | copy-start | bytes 786436
  163.0 658.7 %copy-start.28 = (f32[1024,32]{0,1:T(8,128)S(1)}, f32[1024,32]{0,1:T(8,128)}, u32[]{:S(2)}) copy-start(f32[1024,32]{0,1:T(8,128)} %param.53) | copy-start | bytes 393220
  163.0 658.7 %copy-start.48 = (f32[512,32]{0,1:T(8,128)S(1)}, f32[512,32]{0,1:T(8,128)}, u32[]{:S(2)}) copy-start(f32[512,32]{0,1:T(8,128)} %param.52) | copy-start | bytes 196612
  163.0 658.7 %copy-start.52 = (f32[512,8]{0,1:T(8,128)S(1)}, f32[512,8]{0,1:T(8,128)}, u32[]{:S(2)}) copy-start(f32[512,8]{0,1:T(8,128)} %param.47) | copy-start | bytes 49156
  163.0 658.7 %copy-start.81 = (f32[512,8]{0,1:T(8,128)S(1)}, f32[512,8]{0,1:T(8,128)}, u32[]{:S(2)}) copy-start(f32[512,8]{0,1:T(8,128)} %param.48) | copy-start | bytes 49156
  163.0 658.7 %copy-start.83 = (s32[512,8]{0,1:T(8,128)S(1)}, s32[512,8]{0,1:T(8,128)}, u32[]{:S(2)}) copy-start(s32[512,8]{0,1:T(8,128)} %param.46) | copy-start | bytes 49156
  163.0 658.7 %copy-start.85 = (s32[512,8]{0,1:T(8,128)S(1)}, s32[512,8]{0,1:T(8,128)}, u32[]{:S(2)}) copy-start(s32[512,8]{0,1:T(8,128)} %param.49) | copy-start | bytes 49156
  187.0 634.7 %collective-permute-start.1 = (f32[16,16384]{1,0:T(8,128)}, f32[16,16384]{1,0:T(8,128)S(1)}, u32[]{:S(2)}, u32[]{:S(2)}) collective-permute-start(f32[16,16384]{1,0:T(8,128)} %bitcast.184), channel_id=1, source_target_pairs={{16,0},{17,1},{18,2},{19,3},{20,4},{21,5},{22,6},{23,7},{24,8},{25... | collective-permute-start | bytes 3145736 | tf_op jit(solution)/shard_map/ppermute | solution.py:13
  189.1 11.7 all-to-all-start.3
  193.0 762.1 %reduce-scatter.8.cloned.1.call-start = ((), (), s32[]{:S(2)}) async-start(), calls=%async_computation.12 | async-start | bytes 98304 | tf_op jit(solution)/shard_map/reduce_scatter | solution.py:258
  193.6 761.5 %reduce-scatter.14.cloned.1.call-start = ((), (), s32[]{:S(2)}) async-start(), calls=%async_computation.15 | async-start | bytes 98304 | tf_op jit(solution)/shard_map/reduce_scatter | solution.py:261
  203.8 913.9 %all-reduce.3.cloned.1.call-start = ((), (), s32[]{:S(2)}) async-start(), calls=%async_computation.16 | async-start | bytes 13107200 | tf_op jit(solution)/shard_map/psum | solution.py:237
  947.5 185.3 %reduce-scatter.6.cloned.1.call-start = ((), (), s32[]{:S(2)}) async-start(), calls=%async_computation.11 | async-start | bytes 6291456 | tf_op jit(solution)/shard_map/reduce_scatter | solution.py:257
  948.3 200.8 %reduce-scatter.12.cloned.1.call-start = ((), (), s32[]{:S(2)}) async-start(), calls=%async_computation.14 | async-start | bytes 6291456 | tf_op jit(solution)/shard_map/reduce_scatter | solution.py:260
  1117.7 46.4 %copy-start.37 = (f32[512,512]{1,0:T(8,128)S(1)}, f32[512,512]{1,0:T(8,128)}, u32[]{:S(2)}) copy-start(f32[512,512]{1,0:T(8,128)} %get-tuple-element.1137) | copy-start | bytes 3145732
  1117.7 47.4 %copy-start.25 = (f32[1024,512]{1,0:T(8,128)S(1)}, f32[1024,512]{1,0:T(8,128)}, u32[]{:S(2)}) copy-start(f32[1024,512]{1,0:T(8,128)} %get-tuple-element.1138) | copy-start | bytes 6291460
  (35 other events, 309.6 us)
Sparse Core Ops, SparseCore 0:
  9.7 16.3 all-gather.2
  27.6 14.8 all-gather.4
  188.4 636.5 reduce-scatter.9
  827.6 8.5 reduce-scatter.7
  839.4 8.6 reduce-scatter.13
  947.7 169.9 all-reduce.2
  1120.6 12.1 reduce-scatter.5
  1135.7 13.2 reduce-scatter.11
where the time goes:
time: 1180 us
  waiting for transfers between devices  861 us (73%)
  local copies, waits for them, and re-layouts  110 us (9%)
  matrix products  93.3 us (8%)
  other arithmetic  43.9 us (4%)
  blocking collectives  28.6 us (2%)
  starting transfers between devices  17.3 us (1%)
  between operations  14.9 us (1%)
    ppermute x2, waiting for transfers between devices, shifted(): return lax.ppermute(shard, axis, pairs)  618 us
    psum x1, waiting for transfers between devices, local(): lax.psum((grad_quad_weights[0], grad_quad_weights[1], grad_quad_weights[2...  163 us
    dot_general x14, matrix products, matmul(): jnp.dot(left, right, precision=lax.Precision.HIGHEST, preferred_element_t...  50.3 us
    dot_general x3, matrix products, local_quad(): jnp.einsum('pcd,pce->pde', basis_values, selected_rows, precision=lax.Pre...  43 us
    gather x2, local copies, waits for them, and re-layouts, local_quad(): selected_rows = mixed[indices]  28.9 us
    unnamed x101, local copies, waits for them, and re-layouts  24.3 us
  transfers between devices with their start and end apart: 13, of which 8 were waited for; matrix products, arithmetic and copies ran while one was open for 17% of the time, Pallas kernels for 0%

commit v1 on v0

v1 whole, which is shorter than its diff:
```python
import functools

import jax
import jax.numpy as jnp
from jax import lax
from jax.experimental import pallas as pl
from jax.experimental.pallas import tpu as pltpu
from jax.sharding import PartitionSpec as P

f32, bf16, i32 = jnp.float32, jnp.bfloat16, jnp.int32
root_third = 0.5773502691896258
root_half = 0.7071067811865476
LANES = 128
CLASSES = 4
VMEM_LIMIT = 56 * 2**20


def split(x):
    high = x.astype(bf16)
    return high, (x - high.astype(f32)).astype(bf16)


def dot(left, right, dims):
    return lax.dot_general(left, right, (dims, ((), ())), preferred_element_type=f32)


NN = ((1,), (0,))
NT = ((1,), (1,))
TN = ((0,), (0,))


def dot3(left, right, dims=NN):
    lh, ll = left if isinstance(left, tuple) else split(left)
    rh, rl = right if isinstance(right, tuple) else split(right)
    return dot(lh, rh, dims) + dot(lh, rl, dims) + dot(ll, rh, dims)


def pick(onehot, right, dims=NN):
    rh, rl = right if isinstance(right, tuple) else split(right)
    return dot(onehot, rh, dims) + dot(onehot, rl, dims)


def sigmoid(v):
    return 0.5 * jnp.tanh(0.5 * v) + 0.5


def silu(v):
    return v * sigmoid(v)


def silu_grad(v):
    s = sigmoid(v)
    return s * (1.0 + v * (1.0 - s))


def as_bf16(mask):
    return mask.astype(f32).astype(bf16)


def legendre_steps(cosine, orders):
    before, now = jnp.ones_like(cosine), cosine
    yield before
    yield now
    for order in range(1, orders - 1):
        before, now = now, ((2 * order + 1) / (order + 1)) * cosine * now - (order / (order + 1)) * before
        yield now


def class_table(own, other, classes):
    per = classes // 2
    step = own.shape[1] // per
    parts = []
    for block in (own, other):
        high, low = split(block)
        for q in range(per):
            parts += [high[:, q * step : (q + 1) * step], low[:, q * step : (q + 1) * step]]
    return jnp.concatenate(parts, axis=0)


def gather_classes(table, index, classes, width):
    step = table.shape[1]
    shift = step.bit_length() - 1
    slots = index.shape[1]
    onehot = as_bf16(lax.broadcasted_iota(i32, (step, slots), 0) == (index & (step - 1)))
    found = dot(table, onehot, NN)
    kind = index >> shift
    out = found[0:width] + found[width : 2 * width]
    for q in range(1, classes):
        base = q * 2 * width
        out = jnp.where(kind >= q, found[base : base + width] + found[base + width : base + 2 * width], out)
    return out


def scatter_classes(values, indices, classes, step):
    shift = step.bit_length() - 1
    lefts, rights = [], []
    for value, index in zip(values, indices):
        width, slots = value.shape
        high, low = split(value)
        both = jnp.concatenate([high, low], axis=0)
        kind = jnp.broadcast_to(index >> shift, (2 * width, slots))
        lefts.append(jnp.concatenate([jnp.where(kind == q, both, jnp.zeros((), bf16)) for q in range(classes)], axis=0))
        rights.append(as_bf16(lax.broadcasted_iota(i32, (step, slots), 0) == (index & (step - 1))))
    return dot(jnp.concatenate(lefts, axis=1), jnp.concatenate(rights, axis=1), NT)


def unfold_classes(sums, classes, width):
    parts = []
    for q in range(classes):
        base = q * 2 * width
        parts.append(sums[base : base + width] + sums[base + width : base + 2 * width])
    return jnp.concatenate(parts, axis=1)


def down_kernel(role, own, recv, rbf, w_rad, w_down, emb_out, pre_out, table_out, rad_h, rad_l, down_h, down_l):
    @pl.when(pl.program_id(0) == 0)
    def _():
        rad_h[...], rad_l[...] = split(w_rad[...])
        down_h[...], down_l[...] = split(w_down[...])

    zero = role[0] == 0
    mine, theirs = own[...], recv[...]
    emb = jnp.concatenate([jnp.where(zero, mine, theirs), jnp.where(zero, theirs, mine)], axis=1)
    emb_out[...] = emb
    radial = dot3(rbf[...], (rad_h[...], rad_l[...]))
    mixed = jnp.concatenate([emb, emb], axis=1) * radial
    pre = dot3(mixed, (down_h[...], down_l[...]))
    pre_out[...] = pre
    table_out[...] = silu(pre).T


def quad_forward_kernel(own, other, index, cosine, dihedral, live, w_bil, z_out, rows_out, sel, sel2, basis, *, orders, base):
    slots_k, rows = index.shape
    width = w_bil.shape[1]
    table = class_table(own[base : base + width, :], other[base : base + width, :], 2 * CLASSES)
    alive = live[...].astype(f32)
    for order, series in enumerate(legendre_steps(cosine[...], orders)):
        basis[order] = series * alive
    for k in range(slots_k):
        picked = gather_classes(table, index[k : k + 1, :], 2 * CLASSES, width)
        sel[k] = picked
        sel2[k] = picked * dihedral[k : k + 1, :]
    groups = width // 8
    for t in range(rows // LANES):
        at = slice(t * LANES, (t + 1) * LANES)
        for part, source in enumerate((sel, sel2)):
            for order_at in range(0, orders, 8):
                sums = {}
                for k in range(slots_k):
                    chosen = [source[k, g * 8 : g * 8 + 8, at] for g in range(groups)]
                    for order in range(8):
                        weight = jnp.broadcast_to(basis[order_at + order, k : k + 1, at], (8, LANES))
                        for g in range(groups):
                            term = weight * chosen[g]
                            sums[order, g] = term if k == 0 else sums[order, g] + term
                for (order, g), total in sums.items():
                    row = (part * orders + order_at + order) * width + g * 8
                    z_out[row : row + 8, at] = total
    rows_out[...] = dot3(w_bil[...], z_out[...], TN).T


def triplet_forward_kernel(own, other, index, cosine, live, w_bil, z_out, mid_out, table, sel, basis, bil_h, bil_l, *, orders):
    slots_k, tile = index.shape
    width = w_bil.shape[1]

    @pl.when(pl.program_id(0) == 0)
    def _():
        table[...] = class_table(own[0:width, :], other[0:width, :], CLASSES)
        bil_h[...], bil_l[...] = split(w_bil[...])

    alive = live[...].astype(f32)
    for order, series in enumerate(legendre_steps(cosine[...], orders)):
        basis[order] = series * alive

    def gather_step(k, carry):
        sel[k] = gather_classes(table[...], index[pl.ds(k, 1), :], CLASSES, width)
        return carry

    lax.fori_loop(0, slots_k, gather_step, 0)
    for t in range(tile // LANES):
        at = slice(t * LANES, (t + 1) * LANES)
        for first in range(0, width // 8, 2):
            sums = {}
            for k in range(slots_k):
                chosen = [sel[k, g * 8 : g * 8 + 8, at] for g in (first, first + 1)]
                for order in range(orders):
                    weight = jnp.broadcast_to(basis[order, k : k + 1, at], (8, LANES))
                    for g in range(2):
                        term = weight * chosen[g]
                        sums[order, g] = term if k == 0 else sums[order, g] + term
            for (order, g), total in sums.items():
                row = order * width + (first + g) * 8
                z_out[row : row + 8, at] = total
    mid = dot3((bil_h[...], bil_l[...]), z_out[...], TN)
    mid_out[...] = jnp.concatenate([mid, jnp.zeros_like(mid)], axis=0).T


def rows_by_role(zero, mine, theirs):
    return jnp.concatenate([jnp.where(zero, mine, theirs), jnp.where(zero, theirs, mine)], axis=1)


def pool_of(zero, atom_own, atom_recv, halo_own, halo_recv):
    atoms = rows_by_role(zero, atom_own, atom_recv)
    halo = rows_by_role(zero, halo_own, halo_recv)
    return atoms, jnp.concatenate([atoms, halo], axis=0)


def main_forward_kernel(
    role, emb, mid_trip, rbf, ends, target, quad_rows, atom_own, atom_recv, halo_own, halo_recv,
    w_up, w_one, w_two, w_edge, w_rbf,
    mid_out, joined_out, one_out, two_out, six_out, new_own, new_send, collected,
    up, one, two, three, rad, pool_w, quad_hl,
):
    step = pl.program_id(0)
    tile = emb.shape[0]
    atoms = atom_own.shape[0]
    pool_rows = atoms + halo_own.shape[0]
    atom_width = 2 * atom_own.shape[1]
    zero = role[0] == 0

    @pl.when(step == 0)
    def _():
        up[0], up[1] = split(w_up[...])
        one[0], one[1] = split(w_one[...])
        two[0], two[1] = split(w_two[...])
        three[0], three[1] = split(w_edge[2 * atom_width :, :])
        rad[0], rad[1] = split(w_rbf[...])
        atom_rows, pool = pool_of(zero, atom_own[...], atom_recv[...], halo_own[...], halo_recv[...])
        projected = jnp.concatenate(
            [dot3(pool, w_edge[0:atom_width, :]), dot3(atom_rows, w_edge[atom_width : 2 * atom_width, :])], axis=0
        )
        pool_w[0], pool_w[1] = split(projected)
        high, low = split(quad_rows[...])
        quad_hl[...] = jnp.concatenate([high, low], axis=1)

    own_row = lax.broadcasted_iota(i32, (tile, target.shape[1]), 0) + step * tile
    found = dot(as_bf16(own_row == target[...]), quad_hl[...], NN)
    width = found.shape[1] // 2
    mid = mid_trip[...] + found[:, :width] + found[:, width:]
    mid_out[...] = mid
    joined = (emb[...] + dot3(mid, (up[0], up[1]))) * root_third
    joined_out[...] = joined
    pre_one = dot3(joined, (one[0], one[1]))
    one_out[...] = pre_one
    pre_two = dot3(silu(pre_one), (two[0], two[1]))
    two_out[...] = pre_two
    residual = (joined + silu(pre_two)) * root_half
    row = lax.broadcasted_iota(i32, (pool_rows + atoms, tile), 0)
    member = as_bf16(row == jnp.where(row < pool_rows, ends[0:1, :], ends[1:2, :] + pool_rows))
    pre_six = pick(member, (pool_w[0], pool_w[1]), TN) + dot3(residual, (three[0], three[1]))
    six_out[...] = pre_six
    edge_new = (residual + silu(pre_six)) * root_half
    half = edge_new.shape[1] // 2
    new_own[...] = jnp.where(zero, edge_new[:, :half], edge_new[:, half:])
    new_send[...] = jnp.where(zero, edge_new[:, half:], edge_new[:, :half])
    weighted = edge_new * dot3(rbf[...], (rad[0], rad[1]))
    part = pick(member[pool_rows:, :], weighted)

    @pl.when(step == 0)
    def _():
        collected[...] = part

    @pl.when(step > 0)
    def _():
        collected[...] += part


def main_backward_kernel(
    role, joined, pre_one_ref, pre_two_ref, pre_six_ref, mid_ref, rbf, ends, target, cot_own, cot_recv,
    coll_own, coll_recv, small_own, small_recv, halo_own, halo_recv,
    w_up, w_one, w_two, w_edge, w_rbf, w_edge_atom, w_out,
    sum_grad_out, mid_grad_out, grads, quad_back, pool_grad_own, pool_grad_send, atom_out, feat_out, up_grad,
    up, one, two, three, rad, coll_grad, pool_sum, direct,
    *, scale,
):
    step = pl.program_id(0)
    last = pl.num_programs(0) - 1
    tile = joined.shape[0]
    edge_width = joined.shape[1]
    atoms = small_own.shape[0]
    half = small_own.shape[1] // 3
    atom_width = 2 * half
    pool_rows = atoms + halo_own.shape[0]
    zero = role[0] == 0
    at_edge = 0
    at_two = at_edge + w_edge.shape[0]
    at_one = at_two + edge_width
    at_rbf = at_one + edge_width
    at_atom = at_rbf + w_rbf.shape[0]
    at_last = at_atom + edge_width * atom_width // edge_width

    @pl.when(step == 0)
    def _():
        up[0], up[1] = split(w_up[...])
        one[0], one[1] = split(w_one[...])
        two[0], two[1] = split(w_two[...])
        three[0], three[1] = split(w_edge[2 * atom_width :, :])
        rad[0], rad[1] = split(w_rbf[...])
        mine, theirs = small_own[...], small_recv[...]
        atom_rows = rows_by_role(zero, mine[:, :half], theirs[:, :half])
        cot_atom = rows_by_role(zero, mine[:, half : 2 * half], theirs[:, half : 2 * half])
        cot_feat = rows_by_role(zero, mine[:, 2 * half :], theirs[:, 2 * half :])
        total = (coll_own[...] + coll_recv[...]) * scale
        w_a, w_f = split(w_edge_atom[...]), split(w_out[...])
        pre_atom = dot3(total, w_a)
        atom_new = (atom_rows + silu(pre_atom)) * root_half
        pre_feat = dot3(atom_new, w_f)
        feature = silu(pre_feat)
        atom_out[...] = jnp.where(zero, atom_new[:, :half], atom_new[:, half:])
        feat_out[...] = jnp.where(zero, feature[:, :half], feature[:, half:])
        feat_grad = cot_feat * silu_grad(pre_feat)
        out_grad = 0.5 * dot3(atom_new, feat_grad, TN)
        rows = out_grad.shape[0] // 2
        grads[at_last : at_last + rows, :] = jnp.concatenate([out_grad[:rows], out_grad[rows:]], axis=1)
        atom_grad = (cot_atom + dot3(feat_grad, w_f, NT)) * root_half
        direct[...] = 0.5 * atom_grad
        pre_grad = atom_grad * silu_grad(pre_atom)
        ea_grad = 0.5 * dot3(total, pre_grad, TN)
        rows = ea_grad.shape[0] // 2
        grads[at_atom : at_atom + rows, :] = jnp.concatenate([ea_grad[:rows], ea_grad[rows:]], axis=1)
        coll_grad[0], coll_grad[1] = split(dot3(pre_grad, w_a, NT) * scale)
        grads[0:at_atom, :] = jnp.zeros((at_atom, grads.shape[1]), f32)
        quad_back[...] = jnp.zeros_like(quad_back)
        pool_sum[...] = jnp.zeros_like(pool_sum)
        up_grad[...] = jnp.zeros_like(up_grad)

    row = lax.broadcasted_iota(i32, (pool_rows + atoms, tile), 0)
    member = as_bf16(row == jnp.where(row < pool_rows, ends[0:1, :], ends[1:2, :] + pool_rows))
    joined_now = joined[...]
    pre_two = pre_two_ref[...]
    pre_six = pre_six_ref[...]
    s_two = sigmoid(pre_two)
    s_six = sigmoid(pre_six)
    residual = (joined_now + pre_two * s_two) * root_half
    edge_new = (residual + pre_six * s_six) * root_half
    radial = rbf[...]
    radial_split = split(radial)
    weighted_grad = pick(member[pool_rows:, :], (coll_grad[0], coll_grad[1]), TN)
    grads[at_rbf : at_rbf + rbf.shape[1], :] += dot3(radial_split, weighted_grad * edge_new, TN)
    new_grad = rows_by_role(zero, cot_own[...], cot_recv[...])
    new_grad = (new_grad + weighted_grad * dot3(radial_split, (rad[0], rad[1]))) * root_half
    six_grad = new_grad * (s_six * (1.0 + pre_six * (1.0 - s_six)))
    six_split = split(six_grad)
    pool_sum[...] += pick(member, six_split)
    grads[at_edge + 2 * atom_width : at_two, :] += dot3(residual, six_split, TN)
    res_grad = (new_grad + dot3(six_split, (three[0], three[1]), NT)) * root_half
    two_grad = res_grad * (s_two * (1.0 + pre_two * (1.0 - s_two)))
    two_split = split(two_grad)
    pre_one = pre_one_ref[...]
    s_one = sigmoid(pre_one)
    grads[at_two : at_two + edge_width, :] += dot3(pre_one * s_one, two_split, TN)
    one_grad = dot3(two_split, (two[0], two[1]), NT) * (s_one * (1.0 + pre_one * (1.0 - s_one)))
    one_split = split(one_grad)
    grads[at_one : at_one + edge_width, :] += dot3(joined_now, one_split, TN)
    sum_grad = (res_grad + dot3(one_split, (one[0], one[1]), NT)) * root_third
    sum_grad_out[...] = sum_grad
    sum_split = split(sum_grad)
    up_grad[...] += dot3(mid_ref[...], sum_split, TN)
    mid_grad = dot3(sum_split, (up[0], up[1]), NT)
    mid_grad_out[...] = mid_grad
    own_row = lax.broadcasted_iota(i32, (tile, target.shape[1]), 0) + step * tile
    high, low = split(mid_grad)
    back = dot(as_bf16(own_row == target[...]), jnp.concatenate([high, low], axis=1), TN)
    width = mid_grad.shape[1]
    quad_back[...] += back[:, :width] + back[:, width:]

    @pl.when(step == last)
    def _():
        atom_rows, pool = pool_of(zero, small_own[:, :half], small_recv[:, :half], halo_own[...], halo_recv[...])
        w_src, w_dst = split(w_edge[0:atom_width, :]), split(w_edge[atom_width : 2 * atom_width, :])
        src_split, dst_split = split(pool_sum[0:pool_rows, :]), split(pool_sum[pool_rows:, :])
        grads[at_edge : at_edge + atom_width, :] = dot3(pool, src_split, TN)
        grads[at_edge + atom_width : at_edge + 2 * atom_width, :] = dot3(atom_rows, dst_split, TN)
        from_src = dot3(src_split, w_src, NT)
        from_atoms = from_src[0:atoms] + dot3(dst_split, w_dst, NT) + direct[...]
        result = jnp.concatenate([from_atoms, from_src[atoms:]], axis=0)
        pool_grad_own[...] = jnp.where(zero, result[:, :half], result[:, half:])
        pool_grad_send[...] = jnp.where(zero, result[:, half:], result[:, :half])


def triplet_backward_kernel(mid_grad, z, index, cosine, live, w_bil, bil_grad, table_grad, zg, sg, basis, sums, bil_h, bil_l, *, orders):
    step = pl.program_id(0)
    slots_k, tile = index.shape
    width = w_bil.shape[1]
    classes_step = sums.shape[1]

    @pl.when(step == 0)
    def _():
        bil_h[...], bil_l[...] = split(w_bil[...])
        bil_grad[...] = jnp.zeros_like(bil_grad)
        sums[...] = jnp.zeros_like(sums)

    alive = live[...].astype(f32)
    for order, series in enumerate(legendre_steps(cosine[...], orders)):
        basis[order] = series * alive
    grad = mid_grad[...]
    lane = lax.broadcasted_iota(i32, grad.shape, 1)
    grad = jnp.where(lane < width, grad, 0.0)
    bil_grad[...] += dot3(z[...], grad)
    zg[...] = dot3((bil_h[...], bil_l[...]), grad.T[0:width, :])
    for t in range(tile // LANES):
        at = slice(t * LANES, (t + 1) * LANES)
        for first in range(0, width // 8, 2):
            totals = {}
            for order in range(orders):
                row = order * width + first * 8
                got = [zg[row + g * 8 : row + g * 8 + 8, at] for g in range(2)]
                for k in range(slots_k):
                    weight = jnp.broadcast_to(basis[order, k : k + 1, at], (8, LANES))
                    for g in range(2):
                        term = weight * got[g]
                        totals[k, g] = term if order == 0 else totals[k, g] + term
            for (k, g), total in totals.items():
                sg[k, (first + g) * 8 : (first + g) * 8 + 8, at] = total

    def scatter_step(at, carry):
        first = at * 4
        sums[...] += scatter_classes(
            [sg[first + q] for q in range(4)], [index[pl.ds(first + q, 1), :] for q in range(4)], CLASSES, classes_step
        )
        return carry

    lax.fori_loop(0, slots_k // 4, scatter_step, 0)

    @pl.when(step == pl.num_programs(0) - 1)
    def _():
        table_grad[...] = unfold_classes(sums[...], CLASSES, width)


def quad_backward_kernel(rows_grad, z, index, cosine, dihedral, live, w_bil, bil_grad_in, grads, table_grad, zg, sg, basis, *, orders, base):
    slots_k, rows = index.shape
    width = w_bil.shape[1]
    alive = live[...].astype(f32)
    for order, series in enumerate(legendre_steps(cosine[...], orders)):
        basis[order] = series * alive
    grad = rows_grad[...]
    lane = lax.broadcasted_iota(i32, grad.shape, 1)
    grad = jnp.where((lane >= base) & (lane < base + width), grad, 0.0)
    both = bil_grad_in[...] + dot3(z[...], grad)
    count = both.shape[0] // 4
    grads[...] = jnp.concatenate([both[q * count : (q + 1) * count] for q in range(4)], axis=1)
    zg[...] = dot3(w_bil[...], grad.T[base : base + width, :])
    groups = width // 8
    for t in range(rows // LANES):
        at = slice(t * LANES, (t + 1) * LANES)
        for g in range(groups):
            plain, turned = {}, {}
            for order in range(orders):
                one = zg[order * width + g * 8 : order * width + g * 8 + 8, at]
                two = zg[(orders + order) * width + g * 8 : (orders + order) * width + g * 8 + 8, at]
                for k in range(slots_k):
                    weight = jnp.broadcast_to(basis[order, k : k + 1, at], (8, LANES))
                    plain[k] = weight * one if order == 0 else plain[k] + weight * one
                    turned[k] = weight * two if order == 0 else turned[k] + weight * two
            for k in range(slots_k):
                sg[k, g * 8 : g * 8 + 8, at] = plain[k] + turned[k] * jnp.broadcast_to(dihedral[k : k + 1, at], (8, LANES))
    step = table_grad.shape[1] // (2 * CLASSES)
    sums = scatter_classes([sg[k] for k in range(slots_k)], [index[k : k + 1, :] for k in range(slots_k)], 2 * CLASSES, step)
    table_grad[...] = unfold_classes(sums, 2 * CLASSES, width)


def final_kernel(
    role, emb_ref, rbf, pre_ref, trip_own, trip_recv, quad_own, quad_recv, sum_grad, w_rad, w_down,
    grad_own, grad_send, rad_grad, down_grad,
    rad, down, total,
):
    step = pl.program_id(0)
    zero = role[0] == 0

    @pl.when(step == 0)
    def _():
        rad[0], rad[1] = split(w_rad[...])
        down[0], down[1] = split(w_down[...])
        rad_grad[...] = jnp.zeros_like(rad_grad)
        total[...] = jnp.zeros_like(total)

    emb = emb_ref[...]
    width = emb.shape[1]
    radial_split = split(rbf[...])
    radial = dot3(radial_split, (rad[0], rad[1]))
    doubled = jnp.concatenate([emb, emb], axis=1)
    trip = trip_own[...] + trip_recv[...]
    quad = quad_own[...] + quad_recv[...]
    rest = LANES - trip.shape[0] - quad.shape[0]
    table = jnp.concatenate([trip, quad, jnp.zeros((rest, trip.shape[1]), f32)], axis=0).T
    pre_split = split(table * silu_grad(pre_ref[...]))
    total[...] += dot3(doubled * radial, pre_split, TN)
    mixed_grad = dot3(pre_split, (down[0], down[1]), NT)
    spread = mixed_grad * radial
    grad = sum_grad[...] + spread[:, :width] + spread[:, width:]
    half = width // 2
    grad_own[...] = jnp.where(zero, grad[:, :half], grad[:, half:])
    grad_send[...] = jnp.where(zero, grad[:, half:], grad[:, :half])
    update = dot3(radial_split, mixed_grad * doubled, TN)
    rows = update.shape[0]
    rad_grad[0:rows, :] += update[:, :width]
    rad_grad[rows:, :] += update[:, width:]

    @pl.when(step == pl.num_programs(0) - 1)
    def _():
        lane = lax.broadcasted_iota(i32, (width, LANES), 1)
        both = jnp.where(lane < trip.shape[0], total[0:width, :], total[width:, :])
        count = width // 4
        down_grad[...] = jnp.concatenate([both[q * count : (q + 1) * count] for q in range(4)], axis=1)


def whole(shape):
    return pl.BlockSpec(shape, lambda *_: (0,) * len(shape))


def rows_of(tile, width):
    return pl.BlockSpec((tile, width), lambda i, *_: (i, 0))


def columns_of(rows, tile):
    return pl.BlockSpec((rows, tile), lambda i, *_: (0, i))


def out(*shape):
    return jax.ShapeDtypeStruct(shape, f32)


def call(body, name, grid, in_specs, out_specs, out_shape, scratch, args, scalars=0, flops=0):
    size = sum(a.size * 4 for a in args) + sum(o.size * 4 for o in out_shape)
    return pl.pallas_call(
        body,
        name=name,
        grid_spec=pltpu.PrefetchScalarGridSpec(
            num_scalar_prefetch=scalars, grid=grid, in_specs=in_specs, out_specs=out_specs, scratch_shapes=scratch
        ),
        out_shape=out_shape,
        compiler_params=pltpu.CompilerParams(vmem_limit_bytes=VMEM_LIMIT, dimension_semantics=("arbitrary",) * len(grid)),
        cost_estimate=pl.CostEstimate(flops=flops, bytes_accessed=size, transcendentals=0),
    )(*args)


def swap(x):
    return lax.ppermute(x, "pair", [(0, 1), (1, 0)])


def reduce_everywhere(buffer):
    return lax.psum(buffer, ("pair", "edge"))


def local(
    edge_embed, atom_embed, edge_rbf, edge_src, edge_dst, halo_send, trip_index, trip_cos, trip_live,
    quad_index, quad_cos, quad_dih, quad_live, quad_target,
    w_quad_rbf, w_quad_down, w_quad_bil, w_quad_up, w_trip_rbf, w_trip_down, w_trip_bil, w_trip_up,
    w_res_one, w_res_two, w_atom_edge, w_edge_rbf, w_edge_atom, w_out,
    cot_edge, cot_atom, cot_feat,
):
    peers = lax.axis_size("edge")
    role = lax.axis_index("pair")
    role_arg = role.astype(i32).reshape(1)
    edges, half_width = edge_embed.shape
    half = edges // 2
    width = 2 * half_width
    atoms, half_atom = atom_embed.shape
    radial_width = edge_rbf.shape[1]
    slots = trip_index.shape[1]
    quad_slots = quad_index.shape[1]
    quad_count = quad_index.shape[0]
    half_quad = quad_count // 2
    halo_count = halo_send.shape[0]
    trip_width = w_trip_down.shape[1]
    quad_width = w_quad_down.shape[1]
    orders = w_trip_bil.shape[0] // trip_width
    tile = half // 4
    grid = (half // tile,)
    pad = LANES - trip_width - quad_width

    def own_rows(x, which=role, count=half):
        return lax.dynamic_slice_in_dim(x, which * count, count, axis=0)

    def local_rows(index):
        return jnp.where(role == 0, index, jnp.where(index < half, index + half, index - half))

    emb_recv = swap(own_rows(edge_embed, 1 - role))
    cot_recv = swap(own_rows(cot_edge, 1 - role))
    small_own = jnp.concatenate([atom_embed, cot_atom, cot_feat], axis=1)
    small_recv = swap(small_own)

    w_rad = jnp.concatenate([w_trip_rbf, w_quad_rbf], axis=1)
    w_down = jnp.concatenate(
        [jnp.pad(w_trip_down, ((0, 0), (0, LANES - trip_width))), jnp.pad(w_quad_down, ((0, 0), (trip_width, pad)))], axis=0
    )
    w_up = jnp.concatenate([w_trip_up, w_quad_up, jnp.zeros((pad, width), f32)], axis=0)
    t_index = local_rows(own_rows(trip_index)).T
    t_cos = own_rows(trip_cos).T
    t_live = own_rows(trip_live).T

    def own_quad(x, which=role):
        parts = x.reshape(peers, 2, quad_count // peers // 2, *x.shape[1:])
        return lax.dynamic_index_in_dim(parts, which, axis=1, keepdims=False).reshape(half_quad, *x.shape[1:])

    q_index = local_rows(own_quad(quad_index)).T
    q_cos, q_dih, q_live = (own_quad(x).T for x in (quad_cos, quad_dih, quad_live))
    target = local_rows(jnp.concatenate([own_quad(quad_target), own_quad(quad_target, 1 - role)])).reshape(1, quad_count)
    ends = jnp.stack([own_rows(edge_src), own_rows(edge_dst)])
    halo_out = atom_embed[halo_send].reshape(peers, -1)

    mine = pl.BlockSpec((tile, half_width), lambda i, r: (r[0] * grid[0] + i, 0))
    mine_rbf = pl.BlockSpec((tile, radial_width), lambda i, r: (r[0] * grid[0] + i, 0))
    emb, pre, table = call(
        down_kernel, "down", grid,
        [mine, rows_of(tile, half_width), mine_rbf, whole(w_rad.shape), whole(w_down.shape)],
        [rows_of(tile, width), rows_of(tile, LANES), columns_of(LANES, tile)],
        [out(half, width), out(half, LANES), out(LANES, half)],
        [pltpu.VMEM(w_rad.shape, bf16)] * 2 + [pltpu.VMEM(w_down.shape, bf16)] * 2,
        (role_arg, edge_embed, emb_recv, edge_rbf, w_rad, w_down), scalars=1, flops=6 * half * 2 * width * (radial_width + LANES),
    )
    table_recv = swap(table)

    bil_rows = w_quad_bil.shape[0]
    z_quad, quad_rows = call(
        functools.partial(quad_forward_kernel, orders=orders, base=trip_width), "quad_forward", (1,),
        [whole(table.shape)] * 2 + [whole(q_index.shape)] * 4 + [whole(w_quad_bil.shape)],
        [whole((bil_rows, half_quad)), whole((half_quad, quad_width))],
        [out(bil_rows, half_quad), out(half_quad, quad_width)],
        [pltpu.VMEM((quad_slots, quad_width, half_quad), f32)] * 2 + [pltpu.VMEM((orders, quad_slots, half_quad), f32)],
        (table, table_recv, q_index, q_cos, q_dih, q_live, w_quad_bil), flops=2 * 10**9,
    )
    sent = jnp.concatenate([quad_rows.reshape(peers, -1), halo_out], axis=1)
    cut = quad_rows.size // peers
    routed = lax.all_to_all(sent, "edge", split_axis=0, concat_axis=0, tiled=True)
    routed_recv = swap(routed)

    bil_rows = w_trip_bil.shape[0]
    z_trip, mid_trip = call(
        functools.partial(triplet_forward_kernel, orders=orders), "triplet_forward", grid,
        [whole(table.shape)] * 2 + [columns_of(slots, tile)] * 3 + [whole(w_trip_bil.shape)],
        [columns_of(bil_rows, tile), rows_of(tile, LANES)],
        [out(bil_rows, half), out(half, LANES)],
        [
            pltpu.VMEM((2 * CLASSES * trip_width, edges // CLASSES), bf16),
            pltpu.VMEM((slots, trip_width, tile), f32),
            pltpu.VMEM((orders, slots, tile), f32),
            pltpu.VMEM(w_trip_bil.shape, bf16),
            pltpu.VMEM(w_trip_bil.shape, bf16),
        ],
        (table, table_recv, t_index, t_cos, t_live, w_trip_bil), flops=10 * 10**9,
    )

    quad_all = jnp.concatenate([routed[:, :cut].reshape(half_quad, quad_width), routed_recv[:, :cut].reshape(half_quad, quad_width)], axis=0)
    quad_all = jnp.pad(quad_all, ((0, 0), (trip_width, pad)))
    halo_own = routed[:, cut:].reshape(halo_count, half_atom)
    halo_recv = routed_recv[:, cut:].reshape(halo_count, half_atom)
    atom_recv = small_recv[:, :half_atom]

    pool_rows = atoms + halo_count
    weights_scratch = [
        pltpu.VMEM((2, *w_up.shape), bf16), pltpu.VMEM((2, width, width), bf16), pltpu.VMEM((2, width, width), bf16),
        pltpu.VMEM((2, width, width), bf16), pltpu.VMEM((2, radial_width, width), bf16),
    ]
    mid, joined, pre_one, pre_two, pre_six, new_own, new_send, coll_own = call(
        main_forward_kernel, "main_forward", grid,
        [rows_of(tile, width), rows_of(tile, LANES), mine_rbf, columns_of(2, tile), whole(target.shape), whole(quad_all.shape),
         whole(atom_embed.shape), whole(atom_recv.shape), whole(halo_own.shape), whole(halo_recv.shape),
         whole(w_up.shape), whole(w_res_one.shape), whole(w_res_two.shape), whole(w_atom_edge.shape), whole(w_edge_rbf.shape)],
        [rows_of(tile, LANES)] + [rows_of(tile, width)] * 4 + [rows_of(tile, half_width)] * 2 + [whole((atoms, width))],
        [out(half, LANES)] + [out(half, width)] * 4 + [out(half, half_width)] * 2 + [out(atoms, width)],
        weights_scratch + [pltpu.VMEM((2, pool_rows + atoms, width), bf16), pltpu.VMEM((quad_count, 2 * LANES), bf16)],
        (role_arg, emb, mid_trip, edge_rbf, ends, target, quad_all, atom_embed, atom_recv, halo_own, halo_recv,
         w_up, w_res_one, w_res_two, w_atom_edge, w_edge_rbf), scalars=1, flops=10 * 10**9,
    )
    coll_recv = swap(coll_own)
    new_recv = swap(new_send)

    early_rows = w_atom_edge.shape[0] + 2 * width + radial_width + w_edge_atom.size // width + w_out.size // width
    (sum_grad, mid_grad, early, quad_back, pool_grad_own, pool_grad_send, atom_out, feat_out, up_grad) = call(
        functools.partial(main_backward_kernel, scale=(atoms / edges) ** 0.5), "main_backward", grid,
        [rows_of(tile, width)] * 4 + [rows_of(tile, LANES), mine_rbf, columns_of(2, tile), whole(target.shape), mine, rows_of(tile, half_width),
         whole(coll_own.shape), whole(coll_own.shape), whole(small_own.shape), whole(small_own.shape), whole(halo_own.shape), whole(halo_own.shape),
         whole(w_up.shape), whole(w_res_one.shape), whole(w_res_two.shape), whole(w_atom_edge.shape), whole(w_edge_rbf.shape),
         whole(w_edge_atom.shape), whole(w_out.shape)],
        [rows_of(tile, width), rows_of(tile, LANES), whole((early_rows, width)), whole((quad_count, LANES)),
         whole((pool_rows, half_atom)), whole((pool_rows, half_atom)), whole((atoms, half_atom)), whole((atoms, half_atom)), whole(w_up.shape)],
        [out(half, width), out(half, LANES), out(early_rows, width), out(quad_count, LANES),
         out(pool_rows, half_atom), out(pool_rows, half_atom), out(atoms, half_atom), out(atoms, half_atom), out(*w_up.shape)],
        weights_scratch + [pltpu.VMEM((2, atoms, width), bf16), pltpu.VMEM((pool_rows + atoms, width), f32), pltpu.VMEM((atoms, 2 * half_atom), f32)],
        (role_arg, joined, pre_one, pre_two, pre_six, mid, edge_rbf, ends, target, cot_edge, cot_recv,
         coll_own, coll_recv, small_own, small_recv, halo_own, halo_recv,
         w_up, w_res_one, w_res_two, w_atom_edge, w_edge_rbf, w_edge_atom, w_out), scalars=1, flops=20 * 10**9,
    )
    back_send = jnp.concatenate([quad_back[half_quad:], pool_grad_send], axis=0)
    back_recv = swap(back_send)
    quad_sum = (quad_back[:half_quad] + back_recv[:half_quad])[:, trip_width : trip_width + quad_width]
    pool_grad = pool_grad_own + back_recv[half_quad:]
    returned = jnp.concatenate([quad_sum.reshape(peers, -1), pool_grad[atoms:].reshape(peers, -1)], axis=1)
    returned = lax.all_to_all(returned, "edge", split_axis=0, concat_axis=0, tiled=True)
    early_sum = reduce_everywhere(early)

    bil_grad, trip_table = call(
        functools.partial(triplet_backward_kernel, orders=orders), "triplet_backward", grid,
        [rows_of(tile, LANES), columns_of(bil_rows, tile)] + [columns_of(slots, tile)] * 3 + [whole(w_trip_bil.shape)],
        [whole((bil_rows, LANES)), whole((trip_width, edges))],
        [out(bil_rows, LANES), out(trip_width, edges)],
        [
            pltpu.VMEM((bil_rows, tile), f32),
            pltpu.VMEM((slots, trip_width, tile), f32),
            pltpu.VMEM((orders, slots, tile), f32),
            pltpu.VMEM((2 * CLASSES * trip_width, edges // CLASSES), f32),
            pltpu.VMEM(w_trip_bil.shape, bf16),
            pltpu.VMEM(w_trip_bil.shape, bf16),
        ],
        (mid_grad, z_trip, t_index, t_cos, t_live, w_trip_bil), flops=10 * 10**9,
    )
    rows_grad = jnp.pad(returned[:, :cut].reshape(half_quad, quad_width), ((0, 0), (trip_width, pad)))
    halo_back = returned[:, cut:].reshape(halo_count, half_atom)
    bil_rows = w_quad_bil.shape[0]
    bil_packed, quad_table = call(
        functools.partial(quad_backward_kernel, orders=orders, base=trip_width), "quad_backward", (1,),
        [whole(rows_grad.shape), whole(z_quad.shape)] + [whole(q_index.shape)] * 4 + [whole(w_quad_bil.shape), whole(bil_grad.shape)],
        [whole((bil_rows // 4, 4 * LANES)), whole((quad_width, edges))],
        [out(bil_rows // 4, 4 * LANES), out(quad_width, edges)],
        [pltpu.VMEM((bil_rows, half_quad), f32), pltpu.VMEM((quad_slots, quad_width, half_quad), f32), pltpu.VMEM((orders, quad_slots, half_quad), f32)],
        (rows_grad, z_quad, q_index, q_cos, q_dih, q_live, w_quad_bil, bil_grad), flops=2 * 10**9,
    )
    tables_recv = swap(jnp.concatenate([trip_table[:, half:], quad_table[:, half:]], axis=0))
    trip_recv, quad_recv = tables_recv[:trip_width], tables_recv[trip_width:]

    grad_own, grad_send, rad_grad, down_grad = call(
        final_kernel, "final", grid,
        [rows_of(tile, width), mine_rbf, rows_of(tile, LANES), columns_of(trip_width, tile), columns_of(trip_width, tile),
         columns_of(quad_width, tile), columns_of(quad_width, tile), rows_of(tile, width), whole(w_rad.shape), whole(w_down.shape)],
        [rows_of(tile, half_width)] * 2 + [whole((2 * radial_width, width)), whole((width // 4, 4 * LANES))],
        [out(half, half_width)] * 2 + [out(2 * radial_width, width), out(width // 4, 4 * LANES)],
        [pltpu.VMEM((2, *w_rad.shape), bf16), pltpu.VMEM((2, *w_down.shape), bf16), pltpu.VMEM((2 * width, LANES), f32)],
        (role_arg, emb, edge_rbf, pre, trip_table, trip_recv, quad_table, quad_recv, sum_grad, w_rad, w_down), scalars=1,
        flops=6 * half * 2 * width * (2 * radial_width + 2 * LANES),
    )
    grad_recv = swap(grad_send)
    late = jnp.concatenate([rad_grad, down_grad, bil_packed, up_grad], axis=0)
    late_sum = reduce_everywhere(late)

    def both_halves(own, recv):
        return jnp.where(role == 0, jnp.concatenate([own, recv], axis=0), jnp.concatenate([recv, own], axis=0))

    grad_atom = pool_grad[:atoms] + jnp.zeros((atoms, half_atom), f32).at[halo_send].add(halo_back)

    at = 0
    pieces = []
    for rows in (w_atom_edge.shape[0], width, width, radial_width, w_edge_atom.size // width, w_out.size // width):
        pieces.append(early_sum[at : at + rows])
        at += rows
    g_atom_edge, g_two, g_one, g_edge_rbf, g_ea, g_out = pieces
    atom_width = 2 * half_atom

    def unpack(x, columns):
        return jnp.concatenate([x[:, q * columns : (q + 1) * columns] for q in range(x.shape[1] // columns)], axis=0)

    g_ea, g_out = unpack(g_ea, atom_width), unpack(g_out, atom_width)
    at = 2 * radial_width
    g_trip_rbf, g_quad_rbf = late_sum[:radial_width], late_sum[radial_width:at]
    g_down = unpack(late_sum[at : at + width // 4], LANES)
    at += width // 4
    g_bil = unpack(late_sum[at : at + bil_rows // 4], LANES)
    at += bil_rows // 4
    g_up = late_sum[at:]
    narrow = slice(trip_width, trip_width + quad_width)
    return (
        both_halves(new_own, new_recv), atom_out, feat_out, both_halves(grad_own, grad_recv), grad_atom,
        g_quad_rbf, g_down[:, narrow], g_bil[:, narrow], g_up[narrow],
        g_trip_rbf, g_down[:, :trip_width], g_bil[:, :trip_width], g_up[:trip_width],
        g_one, g_two, g_atom_edge, g_edge_rbf, g_ea, g_out,
    )


def solution(mesh):
    whole_spec, rows_spec, both_spec = P(), P("edge"), P("edge", "pair")
    in_specs = (both_spec, both_spec) + (rows_spec,) * 12 + (whole_spec,) * 14 + (both_spec,) * 3
    out_specs = (both_spec,) * 5 + (whole_spec,) * 14
    return jax.shard_map(local, mesh=mesh, in_specs=in_specs, out_specs=out_specs, check_vma=False)
```

time: 1180 us -> 396 us (0.34)
  waiting for transfers between devices: 861 us -> 167 us
  Pallas kernels: 0 us -> 134 us
  matrix products: 93.3 us -> 0 us
  local copies, waits for them, and re-layouts: 110 us -> 48.7 us
  blocking collectives: 28.6 us -> 0 us
  other arithmetic: 43.9 us -> 15.5 us
    ppermute x2 -> x10, waiting for transfers between devices: 618 us -> 4.69 us  [swap(): return lax.ppermute(x, 'pair', [(0, 1), (1, 0)])]
    pallas_call x0 -> x8, Pallas kernels: none -> 134 us  [call(): pl.pallas_call(body, name=name, grid_spec=pltpu.PrefetchScalarGridSpec(nu...]
    dot_general x17 -> x0, matrix products: 93.3 us -> none  [the longest x14 50.3 us: matmul(): jnp.dot(left, right, precision=lax.Precision.HIGHEST, preferred_element_t...]
    gather x4 -> x1, local copies, waits for them, and re-layouts: 34 us -> 0.64 us  [local(): halo_out = atom_embed[halo_send].reshape(peers, -1)]
    reduce_scatter x5 -> x0, waiting for transfers between devices: 31.4 us -> none  [the longest x1 16.2 us: local(): lax.psum_scatter(grad_embedding + grad_embed_quad, 'pair', scatter_dimens...]
    scatter-add x3 -> x1, other arithmetic: 31.6 us -> 1.29 us  [local(): jnp.zeros((atoms, half_atom), f32).at[halo_send].add(halo_back)]
    all_to_all x3 -> x2, waiting for transfers between devices: 29.5 us -> 5.02 us  [the longest x1 5.02 us: local(): lax.all_to_all(sent, 'edge', split_axis=0, concat_axis=0, tiled=True)]
    all_to_all x1 -> x0, blocking collectives: 22.4 us -> none  [local(): lax.all_to_all(grad_quad_part[quad_target].reshape(partitions, -1), 'edge...]
  transfers between devices with their start and end apart: 13 -> 13, of which waited for: 8 -> 6; matrix products, arithmetic and copies ran while one was open for 17% -> 7% of each run, Pallas kernels for 0% -> 22%
where the time goes in v1:
time: 396 us; the launch traced here: 395 us
  waiting for transfers between devices  167 us (42%)
  Pallas kernels  134 us (34%)
  local copies, waits for them, and re-layouts  48.7 us (12%)
  other arithmetic  15.5 us (4%)
  starting transfers between devices  15.1 us (4%)
  between operations  14.6 us (4%)
    psum x1, waiting for transfers between devices, reduce_everywhere(): return lax.psum(buffer, ('pair', 'edge'))  157 us
    pallas_call x8, Pallas kernels, call(): pl.pallas_call(body, name=name, grid_spec=pltpu.PrefetchScalarGridSpec(nu...  134 us
    unnamed x72, local copies, waits for them, and re-layouts  11.3 us
    all_to_all x1, starting transfers between devices, local(): lax.all_to_all(sent, 'edge', split_axis=0, concat_axis=0, tiled=True)  8.32 us
  transfers between devices with their start and end apart: 13, of which 6 were waited for; matrix products, arithmetic and copies ran while one was open for 7% of the time, Pallas kernels for 22%

profile of v1, /device:TPU:0, one launch (start us, length us, event | category | flops | bytes accessed | tf_op | source)
XLA Modules:
  0.0 394.9 jit_solution(4880066003529105053)
XLA Ops:
  7.2 1.4 constant_dynamic-update-slice_fusion.6
  8.6 1.4 constant_dynamic-update-slice_fusion.5
  10.0 1.4 constant_dynamic-update-slice_fusion.4.small_own
  11.8 1.3 constant_dynamic-slice_fusion
  13.4 1.3 constant_dynamic-slice_fusion.5
  21.5 1.9 copy.102.w_bil
  27.7 7.0 %down.1 = (f32[1024,512]{1,0:T(8,128)}, f32[1024,128]{1,0:T(8,128)}, f32[128,1024]{1,0:T(8,128)}) custom-call(s32[1]{0:T(128)} %bitcast.role, f32[2048,256]{1,0:T(8,128)} %own.1, f32[1024,256]{1,0:T(8,128)} %collective-permute-done.recv, f32[2048,128]{1,0:T(8,128)} %rbf.7, f32[128,1024]{1,0:T(8,128)} %copy-done.12, f32[1024,128]{1,0:T(8,128)} %select_maximum_fusion.w_down), custom_call_target="tpu_custom_call" | custom-call | flops 1610612736 | bytes 8388612 | tf_op jit(solution)/shard_map/down/pallas_call | solution.py:525
  37.7 3.9 quad_forward.1
  43.3 8.3 %all-to-all-start = ((f32[16,1,1536]{2,1,0:T(1,128)}), f32[16,1,1536]{2,1,0:T(1,128)S(1)}, u32[]{:S(2)}, u32[]{:S(2)}) async-start(f32[16,1,1536]{2,1,0:T(1,128)} %all_to_all.16), calls=%async_computation | async-start | bytes 196608 | tf_op jit(solution)/shard_map/all_to_all | solution.py:625
  52.9 1.4 slice.191.atom_recv
  54.3 5.0 %all-to-all-done = f32[16,1,1536]{2,1,0:T(1,128)S(1)} async-done(((f32[16,1,1536]{2,1,0:T(1,128)}), f32[16,1,1536]{2,1,0:T(1,128)S(1)}, u32[]{:S(2)}, u32[]{:S(2)}) %all-to-all-start) | async-done | bytes 98336 | tf_op jit(solution)/shard_map/all_to_all | solution.py:625
  59.4 28.9 %triplet_forward.1 = (f32[1024,1024]{1,0:T(8,128)}, f32[1024,128]{1,0:T(8,128)}) custom-call(f32[128,1024]{1,0:T(8,128)} %get-tuple-element.52.own, f32[128,1024]{1,0:T(8,128)} %copy-done.26, s32[16,1024]{1,0:T(8,128)} %get-tuple-element.182.index, f32[16,1024]{1,0:T(8,128)} %dynamic-slice_bitcast_fusion.1.cosine, s32[16,1024]{1,0:T(8,128)} %get-tuple-element.181.live, ...), custom_call_target="tpu_custom_call" | custom-call | flops 10000000000 | bytes 6225920 | tf_op jit(solution)/shard_map/triplet_forward/pallas_call | solution.py:525
  90.7 20.0 %main_forward.1 = (f32[1024,128]{1,0:T(8,128)}, f32[1024,512]{1,0:T(8,128)}, f32[1024,512]{1,0:T(8,128)}, f32[1024,512]{1,0:T(8,128)}, f32[1024,512]{1,0:T(8,128...) custom-call(s32[1]{0:T(128)} %bitcast.role, f32[1024,512]{1,0:T(8,128)} %get-tuple-element.51.emb.emb_ref, ...), custom_call_target="tpu_custom_call" | custom-call | flops 10000000000 | bytes 19998724 | tf_op jit(solution)/shard_map/main_forward/pallas_call | solution.py:525
  111.2 1.2 collective-permute-done.6.coll_recv
  113.0 30.6 %main_backward.1 = (f32[1024,512]{1,0:T(8,128)}, f32[1024,128]{1,0:T(8,128)}, f32[2560,512]{1,0:T(8,128)}, f32[512,128]{1,0:T(8,128)}, f32[192,128]{1,0:T(8,128)...) custom-call(s32[1]{0:T(128)} %bitcast.role, ...), custom_call_target="tpu_custom_call" | custom-call | flops 20000000000 | bytes 27863044 | tf_op jit(solution)/shard_map/main_backward/pallas_call | solution.py:525
  146.0 1.1 collective-permute-done.7
  149.0 3.5 all-to-all-start.1
  152.6 25.7 %triplet_backward.1 = (f32[1024,128]{1,0:T(8,128)}, f32[64,2048]{1,0:T(8,128)}) custom-call(f32[1024,128]{1,0:T(8,128)} %get-tuple-element.66.mid_grad, f32[1024,1024]{1,0:T(8,128)} %get-tuple-element.67.z, s32[16,1024]{1,0:T(8,128)} %get-tuple-element.182.index, f32[16,1024]{1,0:T(8,128)} %dynamic-slice_bitcast_fusion.1.cosine, ...), custom_call_target="tpu_custom_call" | custom-call | flops 10000000000 | bytes 6225920 | tf_op jit(solution)/shard_map/triplet_backward/pallas_call | solution.py:525
  180.2 5.6 %quad_backward.1 = (f32[256,512]{1,0:T(8,128)}, f32[32,2048]{1,0:T(8,128)}) custom-call(f32[256,128]{1,0:T(8,128)} %pad.18.rows_grad, f32[1024,256]{1,0:T(8,128)} %get-tuple-element.72.z, s32[8,256]{1,0:T(8,128)} %select_bitcast_fusion.1.index, f32[8,256]{1,0:T(8,128)} %bitcast.66, f32[8,256]{1,0:T(8,128)} %bitcast.64, s32[8,256]{1,0:T(8,128)} %bitcast.68, ...), custom_call_target="tpu_custom_call" | custom-call | flops 2000000000 | bytes 2654208 | tf_op jit(solution)/shard_map/quad_backward/pallas_call | solution.py:525
  187.2 1.4 collective-permute-done.8
  189.9 12.6 %final.1 = (f32[1024,256]{1,0:T(8,128)}, f32[1024,256]{1,0:T(8,128)}, f32[256,512]{1,0:T(8,128)}, f32[128,512]{1,0:T(8,128)}) custom-call(s32[1]{0:T(128)} %bitcast.role, f32[1024,512]{1,0:T(8,128)} %get-tuple-element.51.emb.emb_ref, f32[2048,128]{1,0:T(8,128)} %rbf.7, f32[1024,128]{1,0:T(8,128)} %get-tuple-element.65.pre_ref, ...), custom_call_target="tpu_custom_call" | custom-call | flops 3221225472 | bytes 10878980 | tf_op jit(solution)/shard_map/final/pallas_call | solution.py:525
  202.5 2.4 pad_maximum_fusion
  205.6 1.3 scatter_fusion
  207.9 1.6 maximum_select_fusion
  209.5 1.6 maximum_select_fusion.1
  211.0 157.0 %all-reduce.7.cloned.1.call-done = (f32[768,512]{1,0:T(8,128)}, f32[2560,512]{1,0:T(8,128)}) async-done(((f32[768,512]{1,0:T(8,128)}, f32[2560,512]{1,0:T(8,128)}), (f32[768,512]{1,0:T(8,128)}, f32[2560,512]{1,0:T(8,128)})) %all-reduce.7.cloned.1.call-update) | async-done | bytes 6815760 | tf_op jit(solution)/shard_map/psum | solution.py:542
  368.0 1.6 slice.215
  369.6 1.6 slice.219
  372.1 1.7 slice.223
  375.7 1.1 fusion.2
  376.7 3.1 slice.222
  379.8 3.0 fusion.3
  (165 shorter events, 39.6 us)
Async XLA Ops:
  7.2 44.5 %copy-start = (f32[2048,16]{0,1:T(8,128)S(1)}, f32[2048,16]{0,1:T(8,128)}, u32[]{:S(2)}) copy-start(f32[2048,16]{0,1:T(8,128)} %param.38) | copy-start | bytes 393220
  11.4 41.5 %collective-permute-start.3 = (f32[64,384]{1,0:T(8,128)}, f32[64,384]{1,0:T(8,128)}, u32[]{:S(2)}, u32[]{:S(2)}) collective-permute-start(f32[64,384]{1,0:T(8,128)} %constant_dynamic-update-slice_fusion.4.small_own), channel_id=1, source_target_pairs={{0,16},{16,0},{1,17},{17,1},{2,18},{18,2},{3,19},{19,3},{4,20},{20... | collective-permute-start | bytes 294920 | tf_op jit(solution)/shard_map/ppermute | solution.py:538
  11.8 5.3 %copy-start.2 = (f32[64,128]{1,0:T(8,128)S(1)}, f32[64,128]{1,0:T(8,128)}, u32[]{:S(2)}) copy-start(f32[64,128]{1,0:T(8,128)} %atom_own.1) | copy-start | bytes 98308
  11.8 6.0 %copy-start.18 = (s32[512,8]{0,1:T(8,128)S(1)}, s32[512,8]{0,1:T(8,128)}, u32[]{:S(2)}) copy-start(s32[512,8]{0,1:T(8,128)} %param.40) | copy-start | bytes 49156
  11.8 6.2 %copy-start.19 = (f32[512,8]{0,1:T(8,128)S(1)}, f32[512,8]{0,1:T(8,128)}, u32[]{:S(2)}) copy-start(f32[512,8]{0,1:T(8,128)} %param.41) | copy-start | bytes 49156
  13.2 5.1 %copy-start.20 = (f32[512,8]{0,1:T(8,128)S(1)}, f32[512,8]{0,1:T(8,128)}, u32[]{:S(2)}) copy-start(f32[512,8]{0,1:T(8,128)} %param.42) | copy-start | bytes 49156
  13.2 6.8 %copy-start.21 = (s32[512,8]{0,1:T(8,128)S(1)}, s32[512,8]{0,1:T(8,128)}, u32[]{:S(2)}) copy-start(s32[512,8]{0,1:T(8,128)} %param.43) | copy-start | bytes 49156
  13.2 8.0 %copy-start.14 = (f32[512,32]{0,1:T(8,128)S(1)}, f32[512,32]{0,1:T(8,128)}, u32[]{:S(2)}) copy-start(f32[512,32]{0,1:T(8,128)} %param.46) | copy-start | bytes 196612
  13.2 8.1 %copy-start.11 = (f32[512,64]{0,1:T(8,128)S(1)}, f32[512,64]{0,1:T(8,128)}, u32[]{:S(2)}) copy-start(f32[512,64]{0,1:T(8,128)} %param.50) | copy-start | bytes 393220
  13.2 97.9 %collective-permute-start.5 = (f32[1024,256]{1,0:T(8,128)S(1)}, f32[1024,256]{1,0:T(8,128)}, u32[]{:S(2)}, u32[]{:S(2)}) collective-permute-start(f32[1024,256]{1,0:T(8,128)S(1)} %constant_dynamic-slice_fusion), channel_id=1, source_target_pairs={{0,16},{16,0},{1,17},{17,1},{2,18},{18,2},{3,19},{19,3},{4,20},{20... | collective-permute-start | bytes 3145736 | tf_op jit(solution)/shard_map/ppermute | solution.py:538
  14.7 8.7 %copy-start.8 = (f32[1024,64]{0,1:T(8,128)S(1)}, f32[1024,64]{0,1:T(8,128)}, u32[]{:S(2)}) copy-start(f32[1024,64]{0,1:T(8,128)} %param.51) | copy-start | bytes 786436
  14.7 13.0 %collective-permute-start = (f32[1024,256]{1,0:T(8,128)S(1)}, f32[1024,256]{1,0:T(8,128)}, u32[]{:S(2)}, u32[]{:S(2)}) collective-permute-start(f32[1024,256]{1,0:T(8,128)S(1)} %constant_dynamic-slice_fusion.5), channel_id=1, source_target_pairs={{0,16},{16,0},{1,17},{17,1},{2,18},{18,2},{3,19},{19,3},{4,20},{20... | collective-permute-start | bytes 3145736 | tf_op jit(solution)/shard_map/ppermute | solution.py:538
  17.2 8.0 %copy-start.10 = (f32[128,512]{1,0:T(8,128)S(1)}, f32[128,512]{1,0:T(8,128)}, u32[]{:S(2)}) copy-start(f32[128,512]{1,0:T(8,128)} %param.49) | copy-start | bytes 786436
  27.7 7.1 %copy-start.16 = (s32[2048,16]{0,1:T(8,128)S(1)}, s32[2048,16]{0,1:T(8,128)}, u32[]{:S(2)}) copy-start(s32[2048,16]{0,1:T(8,128)} %param.39) | copy-start | bytes 393220
  27.7 7.1 %copy-start.17 = (s32[2048,16]{0,1:T(8,128)S(1)}, s32[2048,16]{0,1:T(8,128)}, u32[]{:S(2)}) copy-start(s32[2048,16]{0,1:T(8,128)} %param.37) | copy-start | bytes 393220
  27.7 8.4 %copy-start.13 = (f32[64,512]{1,0:T(8,128)S(1)}, f32[64,512]{1,0:T(8,128)}, u32[]{:S(2)}) copy-start(f32[64,512]{1,0:T(8,128)} %param.52) | copy-start | bytes 393220
  27.7 8.4 %copy-start.15 = (f32[32,512]{1,0:T(8,128)S(1)}, f32[32,512]{1,0:T(8,128)}, u32[]{:S(2)}) copy-start(f32[32,512]{1,0:T(8,128)} %param.48) | copy-start | bytes 196612
  34.8 2.1 collective-permute-start.1
  37.7 14.6 %dynamic-slice-start = ((s32[2048]{0:T(1024)}, s32[]{:T(128)}), s32[1024]{0:T(1024)S(1)}, s32[]{:S(2)}) async-start(s32[2048]{0:T(1024)} %param.34, s32[]{:T(128)} %select_n.93), calls=%async_computation.3 | async-start | bytes 8704 | tf_op jit(solution)/shard_map/dynamic_slice | solution.py:573
  37.7 14.6 %dynamic-slice-start.1 = ((s32[2048]{0:T(1024)}, s32[]{:T(128)}), s32[1024]{0:T(1024)S(1)}, s32[]{:S(2)}) async-start(s32[2048]{0:T(1024)} %param.35, s32[]{:T(128)} %select_n.93), calls=%async_computation.4 | async-start | bytes 8704 | tf_op jit(solution)/shard_map/dynamic_slice | solution.py:573
  43.3 16.0 %all-to-all-start = ((f32[16,1,1536]{2,1,0:T(1,128)}), f32[16,1,1536]{2,1,0:T(1,128)S(1)}, u32[]{:S(2)}, u32[]{:S(2)}) async-start(f32[16,1,1536]{2,1,0:T(1,128)} %all_to_all.16), calls=%async_computation | async-start | bytes 196608 | tf_op jit(solution)/shard_map/all_to_all | solution.py:625
  59.3 29.7 %collective-permute-start.2 = (f32[16,1536]{1,0:T(8,128)S(1)}, f32[16,1536]{1,0:T(8,128)S(1)}, u32[]{:S(2)}, u32[]{:S(2)}) collective-permute-start(f32[16,1536]{1,0:T(8,128)S(1)} %bitcast.54), channel_id=1, source_target_pairs={{0,16},{16,0},{1,17},{17,1},{2,18},{18,2},{3,19},{19,3},{4,20},{20... | collective-permute-start | bytes 294920 | tf_op jit(solution)/shard_map/ppermute | solution.py:538
  110.6 1.7 collective-permute-start.6
  145.5 1.6 collective-permute-start.7
  149.0 30.2 %all-to-all-start.1 = ((f32[16,1,1536]{2,1,0:T(1,128)}), f32[16,1,1536]{2,1,0:T(1,128)S(1)}, u32[]{:S(2)}, u32[]{:S(2)}) async-start(f32[16,1,1536]{2,1,0:T(1,128)} %all_to_all.19), calls=%async_computation.1 | async-start | bytes 196608 | tf_op jit(solution)/shard_map/all_to_all | solution.py:690
  152.5 215.5 %all-reduce.7.cloned.1.call-start = ((), (), s32[]{:S(2)}) async-start(), calls=%async_computation.2 | async-start | bytes 13631488 | tf_op jit(solution)/shard_map/psum | solution.py:542
  186.7 1.8 collective-permute-start.8
  189.9 12.6 %copy-start.7 = (f32[256,512]{1,0:T(8,128)S(1)}, f32[256,512]{1,0:T(8,128)}, u32[]{:S(2)}) copy-start(f32[256,512]{1,0:T(8,128)} %get-tuple-element.80) | copy-start | bytes 1572868
  189.9 12.6 %copy-start.9 = (f32[128,512]{1,0:T(8,128)S(1)}, f32[128,512]{1,0:T(8,128)}, u32[]{:S(2)}) copy-start(f32[128,512]{1,0:T(8,128)} %get-tuple-element.81) | copy-start | bytes 786436
  204.9 2.9 collective-permute-start.4
  205.4 4.1 %collective-permute-start.9 = (f32[1024,256]{1,0:T(8,128)}, f32[1024,256]{1,0:T(8,128)S(1)}, u32[]{:S(2)}, u32[]{:S(2)}) collective-permute-start(f32[1024,256]{1,0:T(8,128)} %get-tuple-element.77), channel_id=1, source_target_pairs={{0,16},{16,0},{1,17},{17,1},{2,18},{18,2},{3,19},{19,3},{4,20},{20... | collective-permute-start | bytes 3145736 | tf_op jit(solution)/shard_map/ppermute | solution.py:538
  368.0 6.8 %copy-start.4 = (f32[768,512]{1,0:T(8,128)S(1)}, f32[768,512]{1,0:T(8,128)}, u32[]{:S(2)}) copy-start(f32[768,512]{1,0:T(8,128)} %get-tuple-element.161) | copy-start | bytes 4718596
  (12 other events, 26.3 us)
Sparse Core Ops, SparseCore 0:
  205.1 162.8 all-reduce.6

commit v2 on v1

v2 whole, which is shorter than its diff:
```python
import functools

import jax
import jax.numpy as jnp
from jax import lax
from jax.experimental import pallas as pl
from jax.experimental.pallas import tpu as pltpu
from jax.sharding import PartitionSpec as P

f32, bf16, i32 = jnp.float32, jnp.bfloat16, jnp.int32
root_third = 0.5773502691896258
root_half = 0.7071067811865476
LANES = 128
CLASSES = 4
VMEM_LIMIT = 56 * 2**20


def split(x):
    high = x.astype(bf16)
    return high, (x - high.astype(f32)).astype(bf16)


def dot(left, right, dims):
    return lax.dot_general(left, right, (dims, ((), ())), preferred_element_type=f32)


NN = ((1,), (0,))
NT = ((1,), (1,))
TN = ((0,), (0,))


def dot3(left, right, dims=NN):
    lh, ll = left if isinstance(left, tuple) else split(left)
    rh, rl = right if isinstance(right, tuple) else split(right)
    return dot(lh, rh, dims) + dot(lh, rl, dims) + dot(ll, rh, dims)


def pick(onehot, right, dims=NN):
    rh, rl = right if isinstance(right, tuple) else split(right)
    return dot(onehot, rh, dims) + dot(onehot, rl, dims)


def sigmoid(v):
    return 0.5 * jnp.tanh(0.5 * v) + 0.5


def silu(v):
    return v * sigmoid(v)


def silu_grad(v):
    s = sigmoid(v)
    return s * (1.0 + v * (1.0 - s))


def as_bf16(mask):
    return mask.astype(f32).astype(bf16)


def legendre_steps(cosine, orders):
    before, now = jnp.ones_like(cosine), cosine
    yield before
    yield now
    for order in range(1, orders - 1):
        before, now = now, ((2 * order + 1) / (order + 1)) * cosine * now - (order / (order + 1)) * before
        yield now


def class_table(own, other, classes):
    per = classes // 2
    step = own.shape[1] // per
    parts = []
    for block in (own, other):
        high, low = split(block)
        for q in range(per):
            parts += [high[:, q * step : (q + 1) * step], low[:, q * step : (q + 1) * step]]
    return jnp.concatenate(parts, axis=0)


def gather_classes(table, index, classes, width):
    step = table.shape[1]
    shift = step.bit_length() - 1
    slots = index.shape[1]
    onehot = as_bf16(lax.broadcasted_iota(i32, (step, slots), 0) == (index & (step - 1)))
    found = dot(table, onehot, NN)
    kind = index >> shift
    out = found[0:width] + found[width : 2 * width]
    for q in range(1, classes):
        base = q * 2 * width
        out = jnp.where(kind >= q, found[base : base + width] + found[base + width : base + 2 * width], out)
    return out


def scatter_classes(values, indices, classes, step):
    shift = step.bit_length() - 1
    lefts, rights = [], []
    for value, index in zip(values, indices):
        width, slots = value.shape
        high, low = split(value)
        both = jnp.concatenate([high, low], axis=0)
        kind = jnp.broadcast_to(index >> shift, (2 * width, slots))
        lefts.append(jnp.concatenate([jnp.where(kind == q, both, jnp.zeros((), bf16)) for q in range(classes)], axis=0))
        rights.append(as_bf16(lax.broadcasted_iota(i32, (step, slots), 0) == (index & (step - 1))))
    return dot(jnp.concatenate(lefts, axis=1), jnp.concatenate(rights, axis=1), NT)


def unfold_classes(sums, classes, width):
    parts = []
    for q in range(classes):
        base = q * 2 * width
        parts.append(sums[base : base + width] + sums[base + width : base + 2 * width])
    return jnp.concatenate(parts, axis=1)


def joined_halves(zero, mine, theirs, axis=1):
    return jnp.concatenate([jnp.where(zero, mine, theirs), jnp.where(zero, theirs, mine)], axis=axis)


def down_kernel(role, own, recv, rbf, w_trip_rad, w_quad_rad, w_trip, w_quad, emb_out, pre_out, table_out, rad, down_t, down_q):
    width = w_trip_rad.shape[1]

    @pl.when(pl.program_id(0) == 0)
    def _():
        rad[0, :, :width], rad[1, :, :width] = split(w_trip_rad[...])
        rad[0, :, width:], rad[1, :, width:] = split(w_quad_rad[...])
        down_t[0], down_t[1] = split(w_trip[...])
        down_q[0], down_q[1] = split(w_quad[...])

    emb = joined_halves(role[0] == 0, own[...], recv[...])
    emb_out[...] = emb
    radial = dot3(rbf[...], (rad[0], rad[1]))
    pre = jnp.concatenate(
        [
            dot3((down_t[0], down_t[1]), emb * radial[:, :width], NT),
            dot3((down_q[0], down_q[1]), emb * radial[:, width:], NT),
        ],
        axis=0,
    )
    pre_out[...] = pre
    table_out[...] = silu(pre)


def quad_forward_kernel(role, own, other, index, cosine, dihedral, live, w_bil, z_out, rows_out, sel, sel2, basis, *, orders, base):
    slots_k, rows = index.shape
    width = w_bil.shape[0]
    zero = role[0] == 0
    mine, theirs = own[base : base + width, :], other[base : base + width, :]
    table = class_table(jnp.where(zero, mine, theirs), jnp.where(zero, theirs, mine), 2 * CLASSES)
    alive = live[...].astype(f32)
    for order, series in enumerate(legendre_steps(cosine[...], orders)):
        basis[order] = series * alive
    for k in range(slots_k):
        picked = gather_classes(table, index[k : k + 1, :], 2 * CLASSES, width)
        sel[k] = picked
        sel2[k] = picked * dihedral[k : k + 1, :]
    groups = width // 8
    for t in range(rows // LANES):
        at = slice(t * LANES, (t + 1) * LANES)
        for part, source in enumerate((sel, sel2)):
            for order_at in range(0, orders, 8):
                sums = {}
                for k in range(slots_k):
                    chosen = [source[k, g * 8 : g * 8 + 8, at] for g in range(groups)]
                    for order in range(8):
                        weight = jnp.broadcast_to(basis[order_at + order, k : k + 1, at], (8, LANES))
                        for g in range(groups):
                            term = weight * chosen[g]
                            sums[order, g] = term if k == 0 else sums[order, g] + term
                for (order, g), total in sums.items():
                    row = (part * orders + order_at + order) * width + g * 8
                    z_out[row : row + 8, at] = total
    rows_out[...] = dot3(w_bil[...], z_out[...])


def triplet_forward_kernel(role, own, other, index, cosine, live, w_bil, z_out, mid_out, table, sel, basis, bil, *, orders):
    slots_k, tile = index.shape
    width = w_bil.shape[0]

    @pl.when(pl.program_id(0) == 0)
    def _():
        zero = role[0] == 0
        mine, theirs = own[0:width, :], other[0:width, :]
        table[...] = class_table(jnp.where(zero, mine, theirs), jnp.where(zero, theirs, mine), CLASSES)
        bil[0], bil[1] = split(w_bil[...])

    alive = live[...].astype(f32)
    for order, series in enumerate(legendre_steps(cosine[...], orders)):
        basis[order] = series * alive

    def gather(at, k, into):
        where_to = jnp.concatenate([index[k : k + 1, at], index[k + 1 : k + 2, at]], axis=1)
        found = gather_classes(table[...], where_to, CLASSES, width)
        sel[into, k] = found[:, :LANES]
        sel[into, k + 1] = found[:, LANES:]

    def combine(at, first, source):
        sums = {}
        for k in range(slots_k):
            chosen = [sel[source, k, g * 8 : g * 8 + 8, :] for g in (first, first + 1)]
            for order in range(orders):
                weight = jnp.broadcast_to(basis[order, k : k + 1, at], (8, LANES))
                for g in range(2):
                    term = weight * chosen[g]
                    sums[order, g] = term if k == 0 else sums[order, g] + term
        for (order, g), total in sums.items():
            row = order * width + (first + g) * 8
            z_out[row : row + 8, at] = total

    firsts = range(0, width // 8, 2)
    turns = slots_k // 2 // len(firsts)
    columns = lambda c: pl.ds(pl.multiple_of(c * LANES, LANES), LANES)
    for k in range(0, slots_k, 2):
        gather(columns(0), k, 0)

    def step_columns(c, carry):
        for n, first in enumerate(firsts):
            for k in range(n * turns, (n + 1) * turns):
                gather(columns(c), 2 * k, c & 1)
            combine(columns(c - 1), first, 1 - (c & 1))
        return carry

    lax.fori_loop(1, tile // LANES, step_columns, 0)
    for first in firsts:
        combine(columns(tile // LANES - 1), first, (tile // LANES - 1) & 1)
    mid_out[...] = dot3((bil[0], bil[1]), z_out[...])


def edge_members(ends, pool_rows, atoms, tile):
    row = lax.broadcasted_iota(i32, (pool_rows + atoms, tile), 0)
    return as_bf16(row == jnp.where(row < pool_rows, ends[0:1, :], ends[1:2, :] + pool_rows))


def entry_members(role, target, step, tile, half):
    row = lax.broadcasted_iota(i32, (tile, target.shape[1]), 0) + (step * tile + role[0] * half)
    return as_bf16(row == target[...])


def main_forward_kernel(
    role, emb, mid_one, mid_two, rbf, ends, target, quad_own, quad_recv, atom_own, atom_recv, halo_own, halo_recv,
    w_trip_up, w_quad_up, w_one, w_two, w_edge, w_rbf,
    mid_out, joined_out, one_out, two_out, six_out, new_own, new_send, collected,
    up, one, two, three, rad, pool_w, quad_hl,
):
    step = pl.program_id(0)
    tile = emb.shape[0]
    half_rows = tile * pl.num_programs(0)
    atoms = atom_own.shape[0]
    pool_rows = atoms + halo_own.shape[0]
    atom_width = 2 * atom_own.shape[1]
    trip_width = w_trip_up.shape[0]
    zero = role[0] == 0

    @pl.when(step == 0)
    def _():
        up[0, :trip_width], up[1, :trip_width] = split(w_trip_up[...])
        up[0, trip_width:], up[1, trip_width:] = split(w_quad_up[...])
        one[0], one[1] = split(w_one[...])
        two[0], two[1] = split(w_two[...])
        three[0], three[1] = split(w_edge[2 * atom_width :, :])
        rad[0], rad[1] = split(w_rbf[...])
        atom_rows = joined_halves(zero, atom_own[...], atom_recv[...])
        pool = jnp.concatenate([atom_rows, joined_halves(zero, halo_own[...], halo_recv[...])], axis=0)
        projected = jnp.concatenate(
            [dot3(pool, w_edge[0:atom_width, :]), dot3(atom_rows, w_edge[atom_width : 2 * atom_width, :])], axis=0
        )
        pool_w[0], pool_w[1] = split(projected)
        high, low = split(quad_own[...] + quad_recv[...])
        quad_hl[...] = jnp.concatenate([high, low], axis=0)

    found = dot(quad_hl[...], entry_members(role, target, step, tile, half_rows), NT)
    width = found.shape[0] // 2
    mid_trip = jnp.where(step < pl.num_programs(0) // 2, mid_one[...], mid_two[...])
    mid = jnp.concatenate([mid_trip, found[:width] + found[width:]], axis=0)
    mid_out[...] = mid
    joined = (emb[...] + dot3(mid, (up[0], up[1]), TN)) * root_third
    joined_out[...] = joined
    pre_one = dot3(joined, (one[0], one[1]))
    one_out[...] = pre_one
    pre_two = dot3(silu(pre_one), (two[0], two[1]))
    two_out[...] = pre_two
    residual = (joined + silu(pre_two)) * root_half
    member = edge_members(ends, pool_rows, atoms, tile)
    pre_six = pick(member, (pool_w[0], pool_w[1]), TN) + dot3(residual, (three[0], three[1]))
    six_out[...] = pre_six
    edge_new = (residual + silu(pre_six)) * root_half
    half = edge_new.shape[1] // 2
    new_own[...] = jnp.where(zero, edge_new[:, :half], edge_new[:, half:])
    new_send[...] = jnp.where(zero, edge_new[:, half:], edge_new[:, :half])
    weighted = edge_new * dot3(rbf[...], (rad[0], rad[1]))
    part = pick(member[pool_rows:, :], weighted)

    @pl.when(step == 0)
    def _():
        collected[...] = part

    @pl.when(step > 0)
    def _():
        collected[...] += part


def give_halves(place_at, total, keep, send, codes):
    half = keep.shape[0]
    rows = half // len(codes)
    for side, target in ((place_at[0], keep), (1 - place_at[0], send)):
        for n, code in enumerate(codes):
            at = pl.multiple_of(side * half + (place_at[1] ^ code) * rows, 8)
            target[n * rows : (n + 1) * rows, :] = total[pl.ds(at, rows), :]


def side_by_side(x, width):
    parts = width // x.shape[1]
    rows = x.shape[0] // parts
    return jnp.concatenate([x[q * rows : (q + 1) * rows] for q in range(parts)], axis=1)


def edge_backward_kernel(
    role, joined, pre_two_ref, pre_six_ref, rbf, ends, cot_own, cot_recv,
    coll_own, coll_recv, small_own, small_recv, halo_own, halo_recv,
    w_edge, w_rbf, w_edge_atom, w_out,
    res_grad_out, keep, send, pool_grad_own, pool_grad_send, atom_out, feat_out,
    three, rad, coll_grad, pool_sum, direct, grads,
    *, scale, codes,
):
    step = pl.program_id(0)
    last = pl.num_programs(0) - 1
    tile, edge_width = joined.shape
    half = small_own.shape[1]
    atoms = small_own.shape[0] // 3
    atom_width = 2 * half
    pool_rows = atoms + halo_own.shape[0]
    zero = role[0] == 0
    at_rbf = w_edge.shape[0]
    at_atom = at_rbf + w_rbf.shape[0]
    at_last = at_atom + w_edge_atom.shape[0] * atom_width // edge_width
    at_end = at_last + atom_width * atom_width // edge_width

    @pl.when(step == 0)
    def _():
        three[0], three[1] = split(w_edge[2 * atom_width :, :])
        rad[0], rad[1] = split(w_rbf[...])
        mine, theirs = small_own[...], small_recv[...]
        atom_rows = joined_halves(zero, mine[:atoms], theirs[:atoms])
        cot_atom = joined_halves(zero, mine[atoms : 2 * atoms], theirs[atoms : 2 * atoms])
        cot_feat = joined_halves(zero, mine[2 * atoms :], theirs[2 * atoms :])
        total = (coll_own[...] + coll_recv[...]) * scale
        w_a, w_f = split(w_edge_atom[...]), split(w_out[...])
        pre_atom = dot3(total, w_a)
        atom_new = (atom_rows + silu(pre_atom)) * root_half
        pre_feat = dot3(atom_new, w_f)
        feature = silu(pre_feat)
        atom_out[...] = jnp.where(zero, atom_new[:, :half], atom_new[:, half:])
        feat_out[...] = jnp.where(zero, feature[:, :half], feature[:, half:])
        feat_grad = cot_feat * silu_grad(pre_feat)
        grads[at_last:at_end, :] = side_by_side(0.5 * dot3(atom_new, feat_grad, TN), edge_width)
        atom_grad = (cot_atom + dot3(feat_grad, w_f, NT)) * root_half
        direct[...] = 0.5 * atom_grad
        pre_grad = atom_grad * silu_grad(pre_atom)
        grads[at_atom:at_last, :] = side_by_side(0.5 * dot3(total, pre_grad, TN), edge_width)
        coll_grad[0], coll_grad[1] = split(dot3(pre_grad, w_a, NT) * scale)
        grads[0:at_atom, :] = jnp.zeros((at_atom, grads.shape[1]), f32)
        if grads.shape[0] > at_end:
            grads[at_end:, :] = jnp.zeros((grads.shape[0] - at_end, grads.shape[1]), f32)
        pool_sum[...] = jnp.zeros_like(pool_sum)

    member = edge_members(ends, pool_rows, atoms, tile)
    pre_two, pre_six = pre_two_ref[...], pre_six_ref[...]
    s_six = sigmoid(pre_six)
    residual = (joined[...] + silu(pre_two)) * root_half
    edge_new = (residual + pre_six * s_six) * root_half
    radial_split = split(rbf[...])
    weighted_grad = pick(member[pool_rows:, :], (coll_grad[0], coll_grad[1]), TN)
    grads[at_rbf:at_atom, :] += dot3(radial_split, weighted_grad * edge_new, TN)
    new_grad = joined_halves(zero, cot_own[...], cot_recv[...])
    new_grad = (new_grad + weighted_grad * dot3(radial_split, (rad[0], rad[1]))) * root_half
    six_split = split(new_grad * (s_six * (1.0 + pre_six * (1.0 - s_six))))
    pool_sum[...] += pick(member, six_split)
    grads[2 * atom_width : at_rbf, :] += dot3(residual, six_split, TN)
    res_grad_out[...] = (new_grad + dot3(six_split, (three[0], three[1]), NT)) * root_half

    @pl.when(step == last)
    def _():
        atom_rows = joined_halves(zero, small_own[:atoms, :], small_recv[:atoms, :])
        pool = jnp.concatenate([atom_rows, joined_halves(zero, halo_own[...], halo_recv[...])], axis=0)
        w_src, w_dst = split(w_edge[0:atom_width, :]), split(w_edge[atom_width : 2 * atom_width, :])
        src_split, dst_split = split(pool_sum[0:pool_rows, :]), split(pool_sum[pool_rows:, :])
        grads[0:atom_width, :] = dot3(pool, src_split, TN)
        grads[atom_width : 2 * atom_width, :] = dot3(atom_rows, dst_split, TN)
        from_src = dot3(src_split, w_src, NT)
        from_atoms = from_src[0:atoms] + dot3(dst_split, w_dst, NT) + direct[...]
        result = jnp.concatenate([from_atoms, from_src[atoms:]], axis=0)
        pool_grad_own[...] = jnp.where(zero, result[:, :half], result[:, half:])
        pool_grad_send[...] = jnp.where(zero, result[:, half:], result[:, :half])
        give_halves(role, grads, keep, send, codes)


def residual_backward_kernel(
    role, joined, pre_one_ref, pre_two_ref, mid_ref, z_one, z_two, target, res_grad_ref,
    w_trip_up, w_quad_up, w_one, w_two,
    sum_grad_out, mid_grad_out, keep, send, back,
    up, one, two, grads, bil_grad,
    *, codes,
):
    step = pl.program_id(0)
    tile, width = joined.shape
    half_rows = tile * pl.num_programs(0)
    trip_width = w_trip_up.shape[0]
    narrow = up.shape[1]
    at_bil = 2 * width + narrow

    @pl.when(step == 0)
    def _():
        up[0, :trip_width], up[1, :trip_width] = split(w_trip_up[...])
        up[0, trip_width:], up[1, trip_width:] = split(w_quad_up[...])
        one[0], one[1] = split(w_one[...])
        two[0], two[1] = split(w_two[...])
        grads[...] = jnp.zeros_like(grads)
        bil_grad[...] = jnp.zeros_like(bil_grad)
        back[...] = jnp.zeros_like(back)

    blocks = [slice(n * tile // 2, (n + 1) * tile // 2) for n in range(2)]

    def laid(pairs):
        return tuple(jnp.concatenate([p[n] for p in pairs], axis=0) for n in range(2))

    res_grad = [res_grad_ref[at, :] for at in blocks]
    two_split = [split(grad * silu_grad(pre_two_ref[at, :])) for grad, at in zip(res_grad, blocks)]
    pre_one = [pre_one_ref[at, :] for at in blocks]
    s_one = [sigmoid(pre) for pre in pre_one]
    hidden = [split(pre * s) for pre, s in zip(pre_one, s_one)]
    one_split = [
        split(dot3(grad, (two[0], two[1]), NT) * (s * (1.0 + pre * (1.0 - s)))) for grad, pre, s in zip(two_split, pre_one, s_one)
    ]
    grads[0:width, :] += dot3(laid(hidden), laid(two_split), TN)
    sum_grad = [(grad + dot3(inner, (one[0], one[1]), NT)) * root_third for grad, inner in zip(res_grad, one_split)]
    grads[width : 2 * width, :] += dot3(joined[...], laid(one_split), TN)
    for at, grad in zip(blocks, sum_grad):
        sum_grad_out[at, :] = grad
    sum_split = laid([split(grad) for grad in sum_grad])
    grads[2 * width : at_bil, :] += dot3(mid_ref[...], sum_split, NN)
    mid_grad = dot3((up[0], up[1]), sum_split, NT)
    mid_grad_out[...] = mid_grad
    mid_high, mid_low = split(mid_grad)
    z = jnp.where(step < pl.num_programs(0) // 2, z_one[...], z_two[...])
    bil_grad[...] += dot3((mid_high[:trip_width], mid_low[:trip_width]), z, NT)
    found = dot(jnp.concatenate([mid_high[trip_width:], mid_low[trip_width:]], axis=0), entry_members(role, target, step, tile, half_rows), NN)
    rows = narrow - trip_width
    back[...] += found[:rows] + found[rows:]

    @pl.when(step == pl.num_programs(0) - 1)
    def _():
        for q in range(bil_grad.shape[1] // width):
            grads[at_bil + q * trip_width : at_bil + (q + 1) * trip_width, :] = bil_grad[:, q * width : (q + 1) * width]
        give_halves(role, grads, keep, send, codes)


def triplet_backward_kernel(role, mid_grad, index, cosine, live, w_bil, *refs, orders):
    held, (sums, zg, sg, basis, bil) = refs[:-5], refs[-5:]
    step = pl.program_id(0)
    slots_k, tile = index.shape
    width = w_bil.shape[0]
    classes_step = sums.shape[1]

    @pl.when(step == 0)
    def _():
        bil[0], bil[1] = split(w_bil[...])
        sums[...] = held[0][...] if held else jnp.zeros_like(sums)

    alive = live[...].astype(f32)
    for order, series in enumerate(legendre_steps(cosine[...], orders)):
        basis[order] = series * alive
    grad_split = split(mid_grad[0:width, :])
    zg[...] = dot3((bil[0], bil[1]), grad_split, TN)

    def combine(at, first, into):
        totals = {}
        for order in range(orders):
            row = order * width + first * 8
            got = [zg[row + g * 8 : row + g * 8 + 8, at] for g in range(2)]
            for k in range(slots_k):
                weight = jnp.broadcast_to(basis[order, k : k + 1, at], (8, LANES))
                for g in range(2):
                    term = weight * got[g]
                    totals[k, g] = term if order == 0 else totals[k, g] + term
        for (k, g), total in totals.items():
            sg[into, k, (first + g) * 8 : (first + g) * 8 + 8, :] = total

    def scatter(at, first, source):
        slots_at = range(first, first + slots_k // 2)
        sums[...] += scatter_classes(
            [sg[source, k] for k in slots_at], [index[k : k + 1, at] for k in slots_at], CLASSES, classes_step
        )

    firsts = range(0, width // 8, 2)
    columns = lambda c: pl.ds(pl.multiple_of(c * LANES, LANES), LANES)
    for first in firsts:
        combine(columns(0), first, 0)

    def step_columns(c, carry):
        for n, first in enumerate(firsts):
            if n % 2 == 0:
                scatter(columns(c - 1), n // 2 * (slots_k // 2), 1 - (c & 1))
            combine(columns(c), first, c & 1)
        return carry

    lax.fori_loop(1, tile // LANES, step_columns, 0)
    for n in range(2):
        scatter(columns(tile // LANES - 1), n * (slots_k // 2), (tile // LANES - 1) & 1)


def quad_backward_kernel(role, own, z, index, cosine, dihedral, live, w_bil, trip_sums, bil_grad, keep, send, zg, sg, basis, *, orders):
    slots_k, rows = index.shape
    width = w_bil.shape[0]
    edges = trip_sums.shape[1] * CLASSES
    trip_width = trip_sums.shape[0] // (2 * CLASSES)
    zero = role[0] == 0
    alive = live[...].astype(f32)
    for order, series in enumerate(legendre_steps(cosine[...], orders)):
        basis[order] = series * alive
    grad_split = split(own[...])
    bil_grad[...] = dot3(grad_split, z[...], NT)
    zg[...] = dot3(w_bil[...], grad_split, TN)
    groups = width // 8
    for t in range(rows // LANES):
        at = slice(t * LANES, (t + 1) * LANES)
        for g in range(groups):
            plain, turned = {}, {}
            for order in range(orders):
                one = zg[order * width + g * 8 : order * width + g * 8 + 8, at]
                two = zg[(orders + order) * width + g * 8 : (orders + order) * width + g * 8 + 8, at]
                for k in range(slots_k):
                    weight = jnp.broadcast_to(basis[order, k : k + 1, at], (8, LANES))
                    plain[k] = weight * one if order == 0 else plain[k] + weight * one
                    turned[k] = weight * two if order == 0 else turned[k] + weight * two
            for k in range(slots_k):
                sg[k, g * 8 : g * 8 + 8, at] = plain[k] + turned[k] * jnp.broadcast_to(dihedral[k : k + 1, at], (8, LANES))
    step = edges // (2 * CLASSES)
    sums = scatter_classes([sg[k] for k in range(slots_k)], [index[k : k + 1, :] for k in range(slots_k)], 2 * CLASSES, step)
    total = jnp.concatenate([unfold_classes(trip_sums[...], CLASSES, trip_width), unfold_classes(sums, 2 * CLASSES, width)], axis=0)
    half = edges // 2
    keep[...] = jnp.where(zero, total[:, :half], total[:, half:])
    send[...] = jnp.where(zero, total[:, half:], total[:, :half])


def final_kernel(
    role, emb_ref, rbf, pre_ref, table_own, table_recv, sum_grad, quad_bil, w_trip_rad, w_quad_rad, w_trip, w_quad,
    grad_own, grad_send, keep, send,
    rad, down_t, down_q, total,
    *, codes,
):
    step = pl.program_id(0)
    zero = role[0] == 0
    radial_rows, width = w_trip_rad.shape
    trip_width, quad_width = w_trip.shape[0], w_quad.shape[0]
    at_quad_rad = radial_rows
    at_trip = 2 * radial_rows
    at_quad = at_trip + trip_width
    at_quad_bil = at_quad + quad_width
    at_end = at_quad_bil + quad_width * quad_bil.shape[1] // width

    @pl.when(step == 0)
    def _():
        rad[0, :, :width], rad[1, :, :width] = split(w_trip_rad[...])
        rad[0, :, width:], rad[1, :, width:] = split(w_quad_rad[...])
        down_t[0], down_t[1] = split(w_trip[...])
        down_q[0], down_q[1] = split(w_quad[...])
        total[...] = jnp.zeros_like(total)
        rows = quad_bil.shape[0]
        for q in range(quad_bil.shape[1] // width):
            total[at_quad_bil + q * rows : at_quad_bil + (q + 1) * rows, :] = quad_bil[:, q * width : (q + 1) * width]

    emb = emb_ref[...]
    radial_split = split(rbf[...])
    radial = dot3(radial_split, (rad[0], rad[1]))
    pre_grad = (table_own[...] + table_recv[...]) * silu_grad(pre_ref[...])
    trip_split, quad_split = split(pre_grad[:trip_width]), split(pre_grad[trip_width:])
    trip_radial, quad_radial = radial[:, :width], radial[:, width:]
    total[at_trip:at_quad, :] += dot3(trip_split, emb * trip_radial)
    total[at_quad:at_quad_bil, :] += dot3(quad_split, emb * quad_radial)
    trip_mixed = dot3(trip_split, (down_t[0], down_t[1]), TN)
    quad_mixed = dot3(quad_split, (down_q[0], down_q[1]), TN)
    grad = sum_grad[...] + trip_mixed * trip_radial + quad_mixed * quad_radial
    half = width // 2
    grad_own[...] = jnp.where(zero, grad[:, :half], grad[:, half:])
    grad_send[...] = jnp.where(zero, grad[:, half:], grad[:, :half])
    total[0:at_quad_rad, :] += dot3(radial_split, trip_mixed * emb, TN)
    total[at_quad_rad:at_trip, :] += dot3(radial_split, quad_mixed * emb, TN)

    @pl.when(step == pl.num_programs(0) - 1)
    def _():
        give_halves(role, total, keep, send, codes)


def fold_kernel(source, target):
    target[...] = jnp.sum(source[...], axis=0)


def fold(blocks, name, after=()):
    return call(fold_kernel, name, (1,), [whole(blocks.shape)], [whole(blocks.shape[1:])], [out(*blocks.shape[1:])], [], (blocks,), after=after)[0]


def exchange(blocks):
    return lax.all_to_all(blocks, "edge", split_axis=0, concat_axis=0, tiled=True)


def scatter_blocks(rows):
    return exchange(rows.reshape(lax.axis_size("edge"), -1, rows.shape[1]))


def partners(bits, axis="edge"):
    return [(i, i ^ bits) for i in range(lax.axis_size(axis))]


def edge_stages():
    size, shift, stages = lax.axis_size("edge"), 0, []
    while size > 1:
        radix = 8 if size == 8 else 4 if size % 4 == 0 else 2
        stages.append((shift, radix))
        shift += radix.bit_length() - 1
        size //= radix
    return stages


def padded_rows(rows):
    unit = 2 * 8 * lax.axis_size("edge")
    return -(-rows // unit) * unit


def spread(piece, codes, stage):
    shift, radix = stage
    pieces = [piece] + [lax.ppermute(piece, "edge", partners(j << shift)) for j in range(1, radix)]
    return pieces, [[c ^ (j << shift) for c in codes] for j in range(radix)]


def stage_codes(stages):
    codes = [0]
    for shift, radix in reversed(stages):
        codes = [c ^ (j << shift) for j in range(radix) for c in codes]
    return codes


def phase_kernel(*refs, jobs):
    ins, outs = list(refs[: sum(count for _, count, _ in jobs)]), list(refs[sum(count for _, count, _ in jobs) :])
    for kind, count, blocks in jobs:
        parts, ins = ins[:count], ins[count:]
        targets, outs = outs[:blocks], outs[blocks:]
        if kind == "join":
            rows = parts[0].shape[0]
            for n, part in enumerate(parts):
                targets[0][n * rows : (n + 1) * rows, :] = part[...]
        else:
            rows = parts[0].shape[0] // blocks
            for n, target in enumerate(targets):
                total = parts[0][n * rows : (n + 1) * rows, :]
                for part in parts[1:]:
                    total = total + part[n * rows : (n + 1) * rows, :]
                target[...] = total


def phase(jobs, name, after=()):
    ins, shapes = [], []
    for kind, parts, blocks in jobs:
        rows, width = parts[0].shape
        ins += parts
        shapes += [(len(parts) * rows, width)] if kind == "join" else [(rows // blocks, width)] * blocks
    got = call(
        functools.partial(phase_kernel, jobs=[(kind, len(parts), blocks) for kind, parts, blocks in jobs]), name, (1,),
        [whole(x.shape) for x in ins], [whole(x) for x in shapes], [out(*x) for x in shapes], [], tuple(ins), after=after,
    )
    results = []
    for _, _, blocks in jobs:
        results.append(got[:blocks])
        got = got[blocks:]
    return results


def send_blocks(blocks, stage):
    shift, radix = stage
    return [blocks[0]] + [lax.ppermute(blocks[j], "edge", partners(j << shift)) for j in range(1, radix)]


def middle_stages(parts, stages, name):
    for at, stage in enumerate(stages):
        parts = send_blocks(phase([("add", parts, stage[1])], f"{name}{at}")[0], stage)
    return parts


def middle_gathers(piece, stages, name):
    codes = [0]
    for at, stage in enumerate(reversed(stages)):
        pieces, lists = spread(piece, codes, stage)
        piece, codes = phase([("join", pieces, 1)], f"{name}{at}")[0][0], sum(lists, [])
    return piece, codes


def unpack_kernel(place_at, *refs, count, codes, layout):
    ins, outs, total = refs[:count], refs[count:-1], refs[-1]
    half = total.shape[0] // 2
    for n, source in enumerate(ins):
        side, listed = codes[n]
        first = jnp.where(place_at[0] == 0, side, 1 - side) * half
        rows = source.shape[0] // len(listed)
        for at, code in enumerate(listed):
            block = place_at[1] ^ code
            total[pl.ds(pl.multiple_of(first + block * rows, 8), rows), :] = source[at * rows : (at + 1) * rows, :]
    at = 0
    for target, kind in zip(outs, layout):
        height, breadth = target.shape
        width = total.shape[1]
        if kind == "plain":
            target[...] = total[at : at + height, :]
            at += height
        elif kind == "rows":
            parts = width // breadth
            rows = height // parts
            for q in range(parts):
                target[q * rows : (q + 1) * rows, :] = total[at : at + rows, q * breadth : (q + 1) * breadth]
            at += rows
        else:
            for q in range(breadth // width):
                target[:, q * width : (q + 1) * width] = total[at : at + height, :]
                at += height


def unpack(pieces, codes, place_at, shapes, layout, name, after=()):
    count = 2 * len(pieces)
    pieces = pieces + [swap(p) for p in pieces]
    codes = [(0, c) for c in codes] + [(1, c) for c in codes]
    rows = sum(p.shape[0] for p in pieces)
    return call(
        functools.partial(unpack_kernel, count=count, codes=codes, layout=layout), name, (1,), [whole(p.shape) for p in pieces],
        [whole(s) for s in shapes], [out(*s) for s in shapes], [pltpu.VMEM((rows, pieces[0].shape[1]), f32)], (place_at, *pieces), scalars=1, after=after,
    )


def whole(shape):
    return pl.BlockSpec(shape, lambda *_: (0,) * len(shape))


def rows_of(tile, width):
    return pl.BlockSpec((tile, width), lambda i, *_: (i, 0))


def columns_of(rows, tile):
    return pl.BlockSpec((rows, tile), lambda i, *_: (0, i))


def out(*shape):
    return jax.ShapeDtypeStruct(shape, f32)


def call(body, name, grid, in_specs, out_specs, out_shape, scratch, args, scalars=0, flops=0, after=(), aliases={}):
    first, count = len(args), len(after)

    def run(*refs):
        body(*refs[:first], *refs[first + count :])

    args = (*args, *after)
    in_specs = in_specs + [pl.BlockSpec(memory_space=pl.ANY)] * count
    return pl.pallas_call(
        run,
        name=name,
        grid_spec=pltpu.PrefetchScalarGridSpec(
            num_scalar_prefetch=scalars, grid=grid, in_specs=in_specs, out_specs=out_specs, scratch_shapes=scratch
        ),
        out_shape=out_shape,
        compiler_params=pltpu.CompilerParams(vmem_limit_bytes=VMEM_LIMIT, dimension_semantics=("arbitrary",) * len(grid)),
        cost_estimate=pl.CostEstimate(flops=max(flops, 1000), bytes_accessed=1000, transcendentals=0),
        input_output_aliases=aliases,
    )(*args)


def swap(x):
    return lax.ppermute(x, "pair", [(0, 1), (1, 0)])


def local(
    edge_embed, atom_embed, edge_rbf, edge_src, edge_dst, halo_send, trip_index, trip_cos, trip_live,
    quad_index, quad_cos, quad_dih, quad_live, quad_target,
    w_quad_rbf, w_quad_down, w_quad_bil, w_quad_up, w_trip_rbf, w_trip_down, w_trip_bil, w_trip_up,
    w_res_one, w_res_two, w_atom_edge, w_edge_rbf, w_edge_atom, w_out,
    cot_edge, cot_atom, cot_feat,
):
    peers = lax.axis_size("edge")
    role = lax.axis_index("pair")
    role_arg = role.astype(i32).reshape(1)
    place_at = jnp.stack([role, lax.axis_index("edge")]).astype(i32)
    stages = edge_stages()
    plane, line = stages[0], stages[1:]
    codes = stage_codes(stages)
    edges, half_width = edge_embed.shape
    half = edges // 2
    width = 2 * half_width
    atoms, half_atom = atom_embed.shape
    radial_width = edge_rbf.shape[1]
    slots = trip_index.shape[1]
    quad_count, quad_slots = quad_index.shape
    half_quad = quad_count // 2
    halo_count = halo_send.shape[0]
    trip_width = w_trip_down.shape[1]
    quad_width = w_quad_down.shape[1]
    narrow = trip_width + quad_width
    orders = w_trip_bil.shape[0] // trip_width
    atom_width = 2 * half_atom
    tile = half // 2
    grid = (half // tile,)

    def other_rows(x):
        return lax.dynamic_slice_in_dim(x, (1 - role) * half, half, axis=0)

    emb_recv = swap(other_rows(edge_embed))
    cot_recv = swap(other_rows(cot_edge))
    small_own = jnp.concatenate([atom_embed, cot_atom, cot_feat], axis=0)
    small_recv = swap(small_own)
    target = quad_target.reshape(1, quad_count)
    ends = jnp.stack([edge_src, edge_dst])
    halo_out = atom_embed[halo_send].reshape(peers, -1)
    t_index, t_cos, t_live = trip_index.T, trip_cos.T, trip_live.T
    q_index, q_cos, q_dih, q_live = quad_index.T, quad_cos.T, quad_dih.T, quad_live.T
    w_down_t, w_down_q, w_bil_t, w_bil_q = w_trip_down.T, w_quad_down.T, w_trip_bil.T, w_quad_bil.T

    mine = pl.BlockSpec((tile, half_width), lambda i, r: (r[0] * grid[0] + i, 0))
    mine_rbf = pl.BlockSpec((tile, radial_width), lambda i, r: (r[0] * grid[0] + i, 0))
    mine_ends = pl.BlockSpec((2, tile), lambda i, r: (0, r[0] * grid[0] + i))
    mine_slots = pl.BlockSpec((slots, tile), lambda i, r: (0, r[0] * grid[0] + i))
    mine_quad = pl.BlockSpec((quad_slots, half_quad), lambda i, r: (0, r[0]))
    down_scratch = [
        pltpu.VMEM((2, radial_width, 2 * width), bf16), pltpu.VMEM((2, trip_width, width), bf16), pltpu.VMEM((2, quad_width, width), bf16),
    ]
    down_weights = (w_trip_rbf, w_quad_rbf, w_down_t, w_down_q)
    emb, pre, table = call(
        down_kernel, "down", grid,
        [mine, rows_of(tile, half_width), mine_rbf] + [whole(w.shape) for w in down_weights],
        [rows_of(tile, width), columns_of(narrow, tile), columns_of(narrow, tile)],
        [out(half, width), out(narrow, half), out(narrow, half)], down_scratch,
        (role_arg, edge_embed, emb_recv, edge_rbf, *down_weights), scalars=1, flops=4 * 10**9,
    )
    table_recv = swap(table)

    bil_rows = w_bil_q.shape[1]
    z_quad, quad_rows = call(
        functools.partial(quad_forward_kernel, orders=orders, base=trip_width), "quad_forward", (1,),
        [whole(table.shape)] * 2 + [mine_quad] * 4 + [whole(w_bil_q.shape)],
        [whole((bil_rows, half_quad)), whole((quad_width, half_quad))],
        [out(bil_rows, half_quad), out(quad_width, half_quad)],
        [pltpu.VMEM((quad_slots, quad_width, half_quad), f32)] * 2 + [pltpu.VMEM((orders, quad_slots, half_quad), f32)],
        (role_arg, table, table_recv, q_index, q_cos, q_dih, q_live, w_bil_q), scalars=1, flops=2 * 10**9,
    )
    cap = quad_count // peers
    cut = quad_width * cap

    def by_peer(x):
        return x.reshape(quad_width, -1, cap).transpose(1, 0, 2).reshape(-1, cut)

    def by_entry(x):
        return x.reshape(-1, quad_width, cap).transpose(1, 0, 2).reshape(quad_width, -1)

    quad_sent = lax.dynamic_update_slice_in_dim(jnp.zeros((peers, cut), f32), by_peer(quad_rows), role * (peers // 2), axis=0)
    routed = exchange(jnp.concatenate([quad_sent, halo_out], axis=1))
    quad_own = by_entry(routed[:, :cut])
    halo_own = routed[:, cut:].reshape(halo_count, half_atom)
    quad_recv = swap(quad_own)
    halo_recv = swap(halo_own)

    bil_rows = w_bil_t.shape[1]
    steps = grid[0] // 2
    table_shape = (2 * CLASSES * trip_width, edges // CLASSES)

    def halves_of(rows):
        return [
            pl.BlockSpec((rows, tile), lambda i, *_: (0, jnp.minimum(i, steps - 1))),
            pl.BlockSpec((rows, tile), lambda i, *_: (0, jnp.maximum(i - steps, 0))),
        ]

    def slots_at(first):
        return [pl.BlockSpec((slots, tile), lambda i, r: (0, r[0] * grid[0] + first + i))] * 3

    def triplet_forward(first, after):
        return call(
            functools.partial(triplet_forward_kernel, orders=orders), f"triplet_forward{first}", (steps,),
            [whole(table.shape)] * 2 + slots_at(first) + [whole(w_bil_t.shape)],
            [columns_of(bil_rows, tile), columns_of(trip_width, tile)],
            [out(bil_rows, half // 2), out(trip_width, half // 2)],
            [
                pltpu.VMEM(table_shape, bf16),
                pltpu.VMEM((2, slots, trip_width, LANES), f32),
                pltpu.VMEM((orders, slots, tile), f32),
                pltpu.VMEM((2, *w_bil_t.shape), bf16),
            ],
            (role_arg, table, table_recv, t_index, t_cos, t_live, w_bil_t), scalars=1, flops=5 * 10**9, after=after,
        )

    z_one, mid_one = triplet_forward(0, [])
    z_two, mid_two = triplet_forward(steps, [quad_own, halo_own, mid_one])

    atom_recv = small_recv[:atoms]
    pool_rows = atoms + halo_count
    square = pltpu.VMEM((2, width, width), bf16)
    up_scratch = pltpu.VMEM((2, narrow, width), bf16)
    rad_scratch = pltpu.VMEM((2, radial_width, width), bf16)
    main_weights = (w_trip_up, w_quad_up, w_res_one, w_res_two, w_atom_edge, w_edge_rbf)
    main_small = (target, quad_own, quad_recv, atom_embed, atom_recv, halo_own, halo_recv)
    mid, joined, pre_one, pre_two, pre_six, new_own, new_send, coll_own = call(
        main_forward_kernel, "main_forward", grid,
        [rows_of(tile, width), *halves_of(trip_width), mine_rbf, mine_ends]
        + [whole(x.shape) for x in main_small + main_weights],
        [columns_of(narrow, tile)] + [rows_of(tile, width)] * 4 + [mine, rows_of(tile, half_width), whole((atoms, width))],
        [out(narrow, half)] + [out(half, width)] * 4 + [out(edges, half_width), out(half, half_width), out(atoms, width)],
        [up_scratch, square, square, square, rad_scratch, pltpu.VMEM((2, pool_rows + atoms, width), bf16), pltpu.VMEM((2 * quad_width, quad_count), bf16)],
        (role_arg, emb, mid_one, mid_two, edge_rbf, ends, *main_small, *main_weights), scalars=1, flops=8 * 10**9,
    )
    coll_recv = swap(coll_own)
    new_recv = swap(new_send)

    edge_rows = padded_rows(w_atom_edge.shape[0] + radial_width + w_edge_atom.size // width + w_out.size // width)
    atom_args = (coll_own, coll_recv, small_own, small_recv, halo_own, halo_recv, w_atom_edge, w_edge_rbf, w_edge_atom, w_out)
    res_grad, edge_keep, edge_send, pool_grad_own, pool_grad_send, atom_out, feat_out = call(
        functools.partial(edge_backward_kernel, scale=(atoms / edges) ** 0.5, codes=codes), "edge_backward", grid,
        [rows_of(tile, width)] * 3 + [mine_rbf, mine_ends, mine, rows_of(tile, half_width)] + [whole(x.shape) for x in atom_args],
        [rows_of(tile, width), whole((edge_rows // 2, width)), whole((edge_rows // 2, width)),
         whole((pool_rows, half_atom)), whole((pool_rows, half_atom)), whole((atoms, half_atom)), whole((atoms, half_atom))],
        [out(half, width), out(edge_rows // 2, width), out(edge_rows // 2, width),
         out(pool_rows, half_atom), out(pool_rows, half_atom), out(atoms, half_atom), out(atoms, half_atom)],
        [square, rad_scratch, pltpu.VMEM((2, atoms, width), bf16), pltpu.VMEM((pool_rows + atoms, width), f32), pltpu.VMEM((atoms, atom_width), f32),
         pltpu.VMEM((edge_rows, width), f32)],
        (place_at, joined, pre_two, pre_six, edge_rbf, ends, cot_edge, cot_recv, *atom_args), scalars=1, flops=8 * 10**9,
    )
    edge_blocks = phase([("add", [edge_keep, swap(edge_send)], plane[1])], "phase_one")[0]
    edge_parts = middle_stages(send_blocks(edge_blocks, plane), line[:-1], "edge_middle")

    res_rows = padded_rows(2 * width + narrow + w_bil_t.size // width)
    res_weights = (w_trip_up, w_quad_up, w_res_one, w_res_two)
    sum_grad, mid_grad, res_keep, res_send, back_part = call(
        functools.partial(residual_backward_kernel, codes=codes), "residual_backward", grid,
        [rows_of(tile, width)] * 3 + [columns_of(narrow, tile), *halves_of(bil_rows), whole(target.shape), rows_of(tile, width)]
        + [whole(w.shape) for w in res_weights],
        [rows_of(tile, width), columns_of(narrow, tile), whole((res_rows // 2, width)), whole((res_rows // 2, width)), whole((quad_width, quad_count))],
        [out(half, width), out(narrow, half), out(res_rows // 2, width), out(res_rows // 2, width), out(quad_width, quad_count)],
        [up_scratch, square, square, pltpu.VMEM((res_rows, width), f32), pltpu.VMEM(w_bil_t.shape, f32)],
        (place_at, joined, pre_one, pre_two, mid, z_one, z_two, target, res_grad, *res_weights), scalars=1, flops=8 * 10**9, after=edge_blocks,
    )
    sums_shape = (2 * CLASSES * trip_width, edges // CLASSES)

    def triplet_backward(first, held, after):
        return call(
            functools.partial(triplet_backward_kernel, orders=orders), f"triplet_backward{first}", (steps,),
            [pl.BlockSpec((narrow, tile), lambda i, r: (0, first + i))] + slots_at(first) + [whole(w_bil_t.shape)] + [whole(h.shape) for h in held],
            [whole(sums_shape)],
            [out(*sums_shape)],
            [
                pltpu.VMEM((bil_rows, tile), f32),
                pltpu.VMEM((2, slots, trip_width, LANES), f32),
                pltpu.VMEM((orders, slots, tile), f32),
                pltpu.VMEM((2, *w_bil_t.shape), bf16),
            ],
            (role_arg, mid_grad, t_index, t_cos, t_live, w_bil_t, *held), scalars=1, flops=6 * 10**9, after=after,
        )

    edge_blocks, (res_send,), (back_part,), (pool_grad_send,) = phase(
        [("add", edge_parts, line[-1][1]), ("join", [res_send], 1), ("join", [back_part], 1), ("join", [pool_grad_send], 1)], "phase_two", [sum_grad]
    )
    edge_parts = send_blocks(edge_blocks, line[-1])
    res_recv = swap(res_send)
    held = triplet_backward(0, [], edge_blocks)
    (edge_piece,), res_blocks, (pool_grad,), (back_sum,) = phase(
        [
            ("add", edge_parts, 1),
            ("add", [res_keep, res_recv], plane[1]),
            ("add", [pool_grad_own, swap(pool_grad_send)], 1),
            ("add", [back_part, swap(back_part)], 1),
        ],
        "phase_three", held,
    )
    returned_sent = jnp.concatenate([by_peer(back_sum), pool_grad[atoms:].reshape(peers, -1)], axis=1)
    edge_piece, edge_codes = middle_gathers(edge_piece, line[1:], "edge_middle_gather")
    edge_pieces, edge_lists = spread(edge_piece, edge_codes, line[0])
    res_parts = middle_stages(send_blocks(res_blocks, plane), line[:-1], "res_middle")
    returned = exchange(returned_sent)
    (trip_sums,) = triplet_backward(steps, held, [edge_piece, *res_blocks, returned_sent])
    (edge_piece,), res_blocks = phase([("join", edge_pieces, 1), ("add", res_parts, line[-1][1])], "phase_four", [trip_sums])
    edge_pieces, edge_codes = spread(edge_piece, sum(edge_lists, []), plane)
    res_parts = send_blocks(res_blocks, line[-1])
    back_rows = lax.dynamic_slice_in_dim(returned[:, :cut], role * (peers // 2), peers // 2, axis=0)
    back_own = by_entry(back_rows)
    halo_back = returned[:, cut:].reshape(halo_count, half_atom)
    bil_rows = w_bil_q.shape[1]
    quad_bil, table_keep, table_send = call(
        functools.partial(quad_backward_kernel, orders=orders), "quad_backward", (1,),
        [whole(back_own.shape), whole(z_quad.shape)] + [mine_quad] * 4 + [whole(w_bil_q.shape), whole(trip_sums.shape)],
        [whole(w_bil_q.shape), whole((narrow, half)), whole((narrow, half))],
        [out(*w_bil_q.shape), out(narrow, half), out(narrow, half)],
        [pltpu.VMEM((bil_rows, half_quad), f32), pltpu.VMEM((quad_slots, quad_width, half_quad), f32), pltpu.VMEM((orders, quad_slots, half_quad), f32)],
        (role_arg, back_own, z_quad, q_index, q_cos, q_dih, q_live, w_bil_q, trip_sums), scalars=1, flops=2 * 10**9,
        after=[edge_piece, *res_blocks],
    )
    table_recv = swap(table_send)
    ((res_piece,),) = phase([("add", res_parts, 1)], "phase_quad", [table_keep])
    res_piece, res_codes = middle_gathers(res_piece, line[1:], "res_middle_gather")
    res_pieces, res_lists = spread(res_piece, res_codes, line[0])

    late_rows = padded_rows(2 * radial_width + narrow + w_bil_q.size // width)
    grad_own, grad_send, late_keep, late_send = call(
        functools.partial(final_kernel, codes=[0]), "final", grid,
        [rows_of(tile, width), mine_rbf] + [columns_of(narrow, tile)] * 3 + [rows_of(tile, width)]
        + [whole(x.shape) for x in (quad_bil,) + down_weights],
        [mine, rows_of(tile, half_width)] + [whole((late_rows // 2, width))] * 2,
        [out(edges, half_width), out(half, half_width)] + [out(late_rows // 2, width)] * 2,
        down_scratch + [pltpu.VMEM((late_rows, width), f32)],
        (place_at * jnp.array([1, 0], i32), emb, edge_rbf, pre, table_keep, table_recv, sum_grad, quad_bil, *down_weights), scalars=1, flops=6 * 10**9,
        after=[res_piece],
    )
    grad_recv = swap(grad_send)
    (res_piece,), (late_send,) = phase([("join", res_pieces, 1), ("join", [late_send], 1)], "phase_five", edge_pieces[1:])
    ((late_half,),) = phase([("add", [late_keep, swap(late_send)], 1)], "phase_late")
    late_blocks = scatter_blocks(late_half)
    res_pieces, res_codes = spread(res_piece, sum(res_lists, []), plane)
    edge_full = lax.dynamic_update_slice_in_dim(new_own, new_recv, (1 - role) * half, axis=0)
    g_atom_edge, g_edge_rbf, g_edge_atom, g_out = unpack(
        edge_pieces, edge_codes, place_at, [w_atom_edge.shape, w_edge_rbf.shape, w_edge_atom.shape, w_out.shape],
        ["plain", "plain", "rows", "rows"], "edge_unpack", [late_half],
    )
    late_piece = fold(late_blocks, "late_fold", [g_out, *res_pieces])
    late_all = exchange(jnp.broadcast_to(late_piece[None], late_blocks.shape)).reshape(late_half.shape)
    grad_full = lax.dynamic_update_slice_in_dim(grad_own, grad_recv, (1 - role) * half, axis=0)
    g_two, g_one, g_trip_up, g_quad_up, g_bil_t = unpack(
        res_pieces, res_codes, place_at, [w_res_two.shape, w_res_one.shape, w_trip_up.shape, w_quad_up.shape, w_bil_t.shape],
        ["plain"] * 4 + ["columns"], "res_unpack", [late_piece],
    )
    grad_atom = pool_grad[:atoms] + jnp.zeros((atoms, half_atom), f32).at[halo_send].add(halo_back)
    late_all = phase([("join", [late_all], 1)], "phase_six", [g_one, edge_full, grad_full, grad_atom])[0][0]
    g_trip_rbf, g_quad_rbf, g_down_t, g_down_q, g_bil_q = unpack(
        [late_all], [[0]], place_at * jnp.array([1, 0], i32), [w_trip_rbf.shape, w_quad_rbf.shape, w_down_t.shape, w_down_q.shape, w_bil_q.shape],
        ["plain"] * 4 + ["columns"], "late_unpack",
    )
    return (
        edge_full, atom_out, feat_out, grad_full, grad_atom,
        g_quad_rbf, g_down_q.T, g_bil_q.T, g_quad_up, g_trip_rbf, g_down_t.T, g_bil_t.T, g_trip_up,
        g_one, g_two, g_atom_edge, g_edge_rbf, g_edge_atom, g_out,
    )


def solution(mesh):
    whole_spec, rows_spec, both_spec = P(), P("edge"), P("edge", "pair")
    in_specs = (both_spec, both_spec) + (rows_spec,) * 12 + (whole_spec,) * 14 + (both_spec,) * 3
    out_specs = (both_spec,) * 5 + (whole_spec,) * 14
    return jax.shard_map(local, mesh=mesh, in_specs=in_specs, out_specs=out_specs, check_vma=False)
```

time: 396 us -> 294 us (0.74)
  waiting for transfers between devices: 167 us -> 36.5 us
  starting transfers between devices: 15.1 us -> 66.3 us
  local copies, waits for them, and re-layouts: 48.7 us -> 29.2 us
  Pallas kernels: 134 us -> 153 us
  other arithmetic: 15.5 us -> 2.52 us
  between operations: 14.6 us -> 1.74 us
    psum x1 -> x0, waiting for transfers between devices: 157 us -> none  [reduce_everywhere(): return lax.psum(buffer, ('pair', 'edge'))]
    ppermute x0 -> x24, starting transfers between devices: none -> 34.8 us  [the longest x12 18.2 us: send_blocks(): lax.ppermute(blocks[j], 'edge', partners(j << shift))]
    ppermute x0 -> x24, waiting for transfers between devices: none -> 23.1 us  [the longest x12 15.9 us: spread(): lax.ppermute(piece, 'edge', partners(j << shift))]
    slice x23 -> x1, local copies, waits for them, and re-layouts: 20.8 us -> 0.64 us  [local(): atom_recv = small_recv[:atoms]]
    pallas_call x8 -> x23, Pallas kernels: 134 us -> 153 us  [call(): pl.pallas_call(run, name=name, grid_spec=pltpu.PrefetchScalarGridSpec(num...]
    all_to_all x2 -> x4, starting transfers between devices: 11.8 us -> 25.4 us  [exchange(): lax.all_to_all(blocks, 'edge', split_axis=0, concat_axis=0, tiled=True)]
    concatenate x12 -> x1, other arithmetic: 7.53 us -> 0.01 us  [local(): routed = exchange(jnp.concatenate([quad_sent, halo_out], axis=1))]
    ppermute x10 -> x24, waiting for transfers between devices: 4.69 us -> 10.2 us  [swap(): return lax.ppermute(x, 'pair', [(0, 1), (1, 0)])]
  transfers between devices with their start and end apart: 13 -> 52, of which waited for: 6 -> 15; matrix products, arithmetic and copies ran while one was open for 7% -> 5% of each run, Pallas kernels for 22% -> 38%
where the time goes in v2:
time: 294 us; the launch traced here: 289 us
  Pallas kernels  153 us (52%)
  starting transfers between devices  66.3 us (23%)
  waiting for transfers between devices  36.5 us (12%)
  local copies, waits for them, and re-layouts  29.2 us (10%)
    pallas_call x23, Pallas kernels, call(): pl.pallas_call(run, name=name, grid_spec=pltpu.PrefetchScalarGridSpec(num...  153 us
    all_to_all x4, starting transfers between devices, exchange(): lax.all_to_all(blocks, 'edge', split_axis=0, concat_axis=0, tiled=True)  25.4 us
    ppermute x12, starting transfers between devices, send_blocks(): lax.ppermute(blocks[j], 'edge', partners(j << shift))  18.2 us
    ppermute x12, starting transfers between devices, spread(): lax.ppermute(piece, 'edge', partners(j << shift))  16.7 us
    ppermute x12, waiting for transfers between devices, spread(): lax.ppermute(piece, 'edge', partners(j << shift))  15.9 us
    unnamed x147, local copies, waits for them, and re-layouts  14.5 us
    ppermute x24, waiting for transfers between devices, swap(): return lax.ppermute(x, 'pair', [(0, 1), (1, 0)])  10.2 us
    ppermute x12, waiting for transfers between devices, send_blocks(): lax.ppermute(blocks[j], 'edge', partners(j << shift))  7.15 us
  transfers between devices with their start and end apart: 52, of which 15 were waited for; matrix products, arithmetic and copies ran while one was open for 5% of the time, Pallas kernels for 38%

profile of v2, /device:TPU:0, one launch (start us, length us, event | category | flops | bytes accessed | tf_op | source)
XLA Modules:
  0.0 289.1 jit_solution(16194522396441541586)
XLA Ops:
  5.9 6.2 %down.1 = (f32[1024,512]{1,0:T(8,128)}, f32[96,1024]{1,0:T(8,128)}, f32[96,1024]{1,0:T(8,128)}) custom-call(s32[1]{0:T(128)} %bitcast.refs_0_, f32[2048,256]{1,0:T(8,128)} %refs_1_.1, f32[1024,256]{1,0:T(8,128)} %copy-done.58, f32[2048,128]{1,0:T(8,128)} %refs_2_.1, f32[128,512]{1,0:T(8,128)} %refs_8_.1, f32[128,512]{1,0:T(8,128)} %refs_9_.5, ...), custom_call_target="tpu_custom_call" | custom-call | flops 4000000000 | bytes 1000 | tf_op jit(solution)/shard_map/down/pallas_call | solution.py:759
  15.3 3.5 %quad_forward.1 = (f32[1024,256]{1,0:T(8,128)}, f32[32,256]{1,0:T(8,128)}) custom-call(s32[1]{0:T(128)} %bitcast.refs_0_, f32[96,1024]{1,0:T(8,128)} %get-tuple-element.95.refs_1_, f32[96,1024]{1,0:T(8,128)} %copy-done.59, s32[8,512]{1,0:T(8,128)} %bitcast.74, f32[8,512]{1,0:T(8,128)} %bitcast.76, f32[8,512]{1,0:T(8,128)} %bitcast.78, s32[8,512]{1,0:T(8,128)} %bitcast.80, ...), custom_call_target="tpu_custom_call" | custom-call | flops 2000000000 | bytes 1000 | tf_op jit(solution)/shard_map/quad_forward/pallas_call | solution.py:759
  20.6 8.3 %all-to-all-start = ((f32[16,1,2048]{2,1,0:T(1,128)}), f32[16,1,2048]{2,1,0:T(1,128)S(1)}, u32[]{:S(2)}, u32[]{:S(2)}) async-start(f32[16,1,2048]{2,1,0:T(1,128)} %all_to_all.22), calls=%async_computation | async-start | bytes 262144 | tf_op jit(solution)/shard_map/all_to_all | solution.py:602
  28.9 10.0 %triplet_forward0.1 = (f32[1024,512]{1,0:T(8,128)}, f32[64,512]{1,0:T(8,128)}) custom-call(s32[1]{0:T(128)} %bitcast.refs_0_, f32[96,1024]{1,0:T(8,128)} %get-tuple-element.95.refs_1_, f32[96,1024]{1,0:T(8,128)} %copy-done.59, s32[16,2048]{1,0:T(8,128)} %bitcast.53, f32[16,2048]{1,0:T(8,128)} %bitcast.57, s32[16,2048]{1,0:T(8,128)} %bitcast.61, ...), custom_call_target="tpu_custom_call" | custom-call | flops 5000000000 | bytes 1000 | tf_op jit(solution)/shard_map/triplet_forward0/pallas_call | solution.py:759
  40.2 9.9 %triplet_forward1.1 = (f32[1024,512]{1,0:T(8,128)}, f32[64,512]{1,0:T(8,128)}) custom-call(s32[1]{0:T(128)} %bitcast.refs_0_, f32[96,1024]{1,0:T(8,128)} %get-tuple-element.95.refs_1_, f32[96,1024]{1,0:T(8,128)} %copy-done.59, s32[16,2048]{1,0:T(8,128)} %bitcast.54, f32[16,2048]{1,0:T(8,128)} %bitcast.58, s32[16,2048]{1,0:T(8,128)} %bitcast.62, ...), custom_call_target="tpu_custom_call" | custom-call | flops 5000000000 | bytes 1000 | tf_op jit(solution)/shard_map/triplet_forward1/pallas_call | solution.py:759
  50.8 16.6 %main_forward.1 = (f32[96,1024]{1,0:T(8,128)}, f32[1024,512]{1,0:T(8,128)}, f32[1024,512]{1,0:T(8,128)}, f32[1024,512]{1,0:T(8,128)}, f32[1024,512]{1,0:T(8,128)...) custom-call(s32[1]{0:T(128)} %bitcast.refs_0_, f32[1024,512]{1,0:T(8,128)} %get-tuple-element.94.refs_1_, ...), custom_call_target="tpu_custom_call" | custom-call | flops 8000000000 | bytes 1000 | tf_op jit(solution)/shard_map/main_forward/pallas_call | solution.py:759
  69.7 17.6 %edge_backward.1 = (f32[1024,512]{1,0:T(8,128)}, f32[768,512]{1,0:T(8,128)}, f32[768,512]{1,0:T(8,128)}, f32[192,128]{1,0:T(8,128)}, f32[192,128]{1,0:T(8,128)}, /*index=5*/f32[64,128]{1,0:T(8,128)}, f32[64,128]{1,0:T(8,128)}) custom-call(s32[2]{0:T(128)} %get-tuple-element.170.refs_0_, f32[1024,512]{1,0:T(8,128)} %get-tuple-element.101.refs_1_, ...), custom_call_target="tpu_custom_call" | custom-call | flops 8000000000 | bytes 1000 | tf_op jit(solution)/shard_map/edge_backward/pallas_call | solution.py:759
  87.8 3.2 %collective-permute-done.8.refs_1_ = f32[768,512]{1,0:T(8,128)S(1)} collective-permute-done((f32[768,512]{1,0:T(8,128)}, f32[768,512]{1,0:T(8,128)S(1)}, u32[]{:S(2)}, u32[]{:S(2)}) %collective-permute-start.8) | collective-permute-done | bytes 1572896 | tf_op jit(solution)/shard_map/ppermute | solution.py:773
  92.2 3.1 %phase_one.1 = (f32[192,512]{1,0:T(8,128)}, f32[192,512]{1,0:T(8,128)}, f32[192,512]{1,0:T(8,128)}, f32[192,512]{1,0:T(8,128)}) custom-call(f32[768,512]{1,0:T(8,128)} %get-tuple-element.108.refs_0_, f32[768,512]{1,0:T(8,128)} %copy-done.6), custom_call_target="tpu_custom_call" | custom-call | flops 1000 | bytes 1000 | tf_op jit(solution)/shard_map/phase_one/pallas_call | solution.py:759
  98.8 18.7 %residual_backward.1 = (f32[1024,512]{1,0:T(8,128)}, f32[96,1024]{1,0:T(8,128)}, f32[640,512]{1,0:T(8,128)}, f32[640,512]{1,0:T(8,128)}, f32[32,512]{1,0:T(8,128)}) custom-call(s32[2]{0:T(128)} %get-tuple-element.170.refs_0_, f32[1024,512]{1,0:T(8,128)} %get-tuple-element.101.refs_1_, f32[1024,512]{1,0:T(8,128)} %get-tuple-element.114.refs_2_, ...), custom_call_target="tpu_custom_call" | custom-call | flops 8000000000 | bytes 1000 | tf_op jit(solution)/shard_map/residual_backward/pallas_call | solution.py:759
  118.6 3.1 %phase_two.1 = (f32[48,512]{1,0:T(8,128)}, f32[48,512]{1,0:T(8,128)}, f32[48,512]{1,0:T(8,128)}, f32[48,512]{1,0:T(8,128)}, f32[640,512]{1,0:T(8,128)}, /*index=5*/f32[32,512]{1,0:T(8,128)}, f32[192,128]{1,0:T(8,128)}) custom-call(f32[192,512]{1,0:T(8,128)} %get-tuple-element.110.refs_13_.refs_0_, f32[192,512]{1,0:T(8,128)} %copy-done.19, ...), custom_call_target="tpu_custom_call" | custom-call | flops 1000 | bytes 1000 | tf_op jit(solution)/shard_map/phase_two/pallas_call | solution.py:759
  124.2 2.4 collective-permute-start.13
  128.8 10.8 %triplet_backward0.1.refs_10_.refs_6_ = f32[512,512]{1,0:T(8,128)} custom-call(s32[1]{0:T(128)} %bitcast.refs_0_, f32[96,1024]{1,0:T(8,128)} %get-tuple-element.132.refs_1_, s32[16,2048]{1,0:T(8,128)} %bitcast.55, f32[16,2048]{1,0:T(8,128)} %bitcast.59, s32[16,2048]{1,0:T(8,128)} %bitcast.63, f32[64,1024]{1,0:T(8,128)} %bitcast.50, ...), custom_call_target="tpu_custom_call" | custom-call | flops 6000000000 | bytes 1000 | tf_op jit(solution)/shard_map/triplet_backward0/pallas_call | solution.py:759
  140.8 3.1 %phase_three.1 = (f32[48,512]{1,0:T(8,128)}, f32[160,512]{1,0:T(8,128)}, f32[160,512]{1,0:T(8,128)}, f32[160,512]{1,0:T(8,128)}, f32[160,512]{1,0:T(8,128)}, /*index=5*/f32[192,128]{1,0:T(8,128)}, f32[32,512]{1,0:T(8,128)}) custom-call(f32[48,512]{1,0:T(8,128)} %get-tuple-element.123.refs_6_.refs_0_, f32[48,512]{1,0:T(8,128)} %copy-done.38, ...), custom_call_target="tpu_custom_call" | custom-call | flops 1000 | bytes 1000 | tf_op jit(solution)/shard_map/phase_three/pallas_call | solution.py:759
  148.4 6.3 %all-to-all-start.1 = ((f32[16,1,2048]{2,1,0:T(1,128)}), f32[16,1,2048]{2,1,0:T(1,128)S(1)}, u32[]{:S(2)}, u32[]{:S(2)}) async-start(f32[16,1,2048]{2,1,0:T(1,128)} %copy.62), calls=%async_computation.1 | async-start | bytes 262144 | tf_op jit(solution)/shard_map/all_to_all | solution.py:602
  158.4 11.2 %triplet_backward1.1.refs_8_ = f32[512,512]{1,0:T(8,128)} custom-call(s32[1]{0:T(128)} %bitcast.refs_0_, f32[96,1024]{1,0:T(8,128)} %get-tuple-element.132.refs_1_, s32[16,2048]{1,0:T(8,128)} %bitcast.56, f32[16,2048]{1,0:T(8,128)} %bitcast.60, s32[16,2048]{1,0:T(8,128)} %bitcast.64, f32[64,1024]{1,0:T(8,128)} %bitcast.51, ...), custom_call_target="tpu_custom_call" | custom-call | flops 6000000000 | bytes 1000 | tf_op jit(solution)/shard_map/triplet_backward1/pallas_call | solution.py:759
  178.2 5.6 %quad_backward.1 = (f32[32,1024]{1,0:T(8,128)}, f32[96,1024]{1,0:T(8,128)}, f32[96,1024]{1,0:T(8,128)}) custom-call(s32[1]{0:T(128)} %bitcast.refs_0_, f32[32,256]{1,0:T(8,128)} %reshape.103.refs_1_, f32[1024,256]{1,0:T(8,128)} %get-tuple-element.135.refs_2_, s32[8,512]{1,0:T(8,128)} %bitcast.75, f32[8,512]{1,0:T(8,128)} %bitcast.77, f32[8,512]{1,0:T(8,128)} %bitcast.79, ...), custom_call_target="tpu_custom_call" | custom-call | flops 2000000000 | bytes 1000 | tf_op jit(solution)/shard_map/quad_backward/pallas_call | solution.py:759
  185.9 2.4 collective-permute-start.26
  189.0 6.5 %collective-permute-done.26.refs_2_ = f32[40,512]{1,0:T(8,128)S(1)} collective-permute-done((f32[40,512]{1,0:T(8,128)S(1)}, f32[40,512]{1,0:T(8,128)S(1)}, u32[]{:S(2)}, u32[]{:S(2)}) %collective-permute-start.26) | collective-permute-done | bytes 81952 | tf_op jit(solution)/shard_map/ppermute | solution.py:678
  197.8 2.5 collective-permute-start.31
  200.3 2.4 collective-permute-start.34
  205.0 2.3 collective-permute-start.29
  207.4 10.5 %final.1 = (f32[2048,256]{1,0:T(8,128)}, f32[1024,256]{1,0:T(8,128)}, f32[256,512]{1,0:T(8,128)}, f32[256,512]{1,0:T(8,128)}) custom-call(s32[2]{0:T(128)} %get-tuple-element.169.refs_0_, f32[1024,512]{1,0:T(8,128)} %get-tuple-element.94.refs_1_, f32[2048,128]{1,0:T(8,128)} %refs_2_.1, f32[96,1024]{1,0:T(8,128)} %get-tuple-element.107.refs_3_, ...), custom_call_target="tpu_custom_call" | custom-call | flops 6000000000 | bytes 1000 | tf_op jit(solution)/shard_map/final/pallas_call | solution.py:759
  226.1 5.2 %all-to-all-start.2 = ((f32[16,16,512]{2,1,0:T(8,128)}), f32[16,16,512]{2,1,0:T(8,128)S(1)}, u32[]{:S(2)}, u32[]{:S(2)}) async-start(f32[16,16,512]{2,1,0:T(8,128)} %bitcast.37), calls=%async_computation.2 | async-start | bytes 1048576 | tf_op jit(solution)/shard_map/all_to_all | solution.py:602
  233.1 2.9 %collective-permute-start.42 = (f32[160,512]{1,0:T(8,128)}, f32[160,512]{1,0:T(8,128)S(1)}, u32[]{:S(2)}, u32[]{:S(2)}) collective-permute-start(f32[160,512]{1,0:T(8,128)} %get-tuple-element.155.refs_2_.refs_1_), channel_id=1, source_target_pairs={{0,3},{1,2},{2,1},{3,0},{4,7},{5,6},{6,5},{7,4},{8,11},{9,10},{10,... | collective-permute-start | bytes 983048 | tf_op jit(solution)/shard_map/ppermute | solution.py:630
  237.9 4.4 %edge_unpack.1 = (f32[1024,512]{1,0:T(8,128)}, f32[128,512]{1,0:T(8,128)}, f32[512,256]{1,0:T(8,128)}, f32[256,256]{1,0:T(8,128)}) custom-call(s32[2]{0:T(128)} %get-tuple-element.170.refs_0_, f32[192,512]{1,0:T(8,128)} %get-tuple-element.141.refs_9_.refs_1_, f32[192,512]{1,0:T(8,128)} %copy-done.11, f32[192,512]{1,0:T(8,128)} %copy-done.9, ...), custom_call_target="tpu_custom_call" | custom-call | flops 1000 | bytes 1000 | tf_op jit(solution)/shard_map/edge_unpack/pallas_call | solution.py:759
  242.4 6.5 %collective-permute-done.42.refs_5_.refs_4_ = f32[160,512]{1,0:T(8,128)S(1)} collective-permute-done((f32[160,512]{1,0:T(8,128)}, f32[160,512]{1,0:T(8,128)S(1)}, u32[]{:S(2)}, u32[]{:S(2)}) %collective-permute-start.42) | collective-permute-done | bytes 327712 | tf_op jit(solution)/shard_map/ppermute | solution.py:630
  248.9 5.4 %collective-permute-done.41.refs_4_.refs_3_ = f32[160,512]{1,0:T(8,128)S(1)} collective-permute-done((f32[160,512]{1,0:T(8,128)}, f32[160,512]{1,0:T(8,128)S(1)}, u32[]{:S(2)}, u32[]{:S(2)}) %collective-permute-start.41) | collective-permute-done | bytes 327712 | tf_op jit(solution)/shard_map/ppermute | solution.py:630
  259.8 5.6 %all-to-all-start.3 = ((f32[16,16,512]{2,1,0:T(8,128)}), f32[16,16,512]{2,1,0:T(8,128)S(1)}, u32[]{:S(2)}, u32[]{:S(2)}) async-start(f32[16,16,512]{2,1,0:T(8,128)} %broadcast_in_dim.16), calls=%async_computation.3 | async-start | bytes 1048576 | tf_op jit(solution)/shard_map/all_to_all | solution.py:602
  273.1 4.0 %res_unpack.1 = (f32[512,512]{1,0:T(8,128)}, f32[512,512]{1,0:T(8,128)}, f32[64,512]{1,0:T(8,128)}, f32[32,512]{1,0:T(8,128)}, f32[64,1024]{1,0:T(8,128)}) custom-call(s32[2]{0:T(128)} %get-tuple-element.170.refs_0_, f32[160,512]{1,0:T(8,128)} %get-tuple-element.155.refs_2_.refs_1_, f32[160,512]{1,0:T(8,128)} %collective-permute-done.40.refs_3_.refs_2_, ...), custom_call_target="tpu_custom_call" | custom-call | flops 1000 | bytes 1000 | tf_op jit(solution)/shard_map/res_unpack/pallas_call | solution.py:759
  277.2 3.2 %all-to-all-done.3 = f32[16,16,512]{2,1,0:T(8,128)S(1)} async-done(((f32[16,16,512]{2,1,0:T(8,128)}), f32[16,16,512]{2,1,0:T(8,128)S(1)}, u32[]{:S(2)}, u32[]{:S(2)}) %all-to-all-start.3) | async-done | bytes 524320 | tf_op jit(solution)/shard_map/all_to_all | solution.py:602
  286.0 2.8 late_unpack.1
  (282 shorter events, 81.1 us)
Async XLA Ops:
  2.7 11.2 %collective-permute-start.3 = (f32[192,128]{1,0:T(8,128)S(1)}, f32[192,128]{1,0:T(8,128)S(1)}, u32[]{:S(2)}, u32[]{:S(2)}) collective-permute-start(f32[192,128]{1,0:T(8,128)S(1)} %constant_dynamic-update-slice_fusion.refs_10_), channel_id=1, source_target_pairs={{0,16},{16,0},{1,17},{17,1},{2,18},{18,2},{3,19},{19,3},{4,20},{20... | collective-permute-start | bytes 294920 | tf_op jit(solution)/shard_map/ppermute | solution.py:773
  2.9 65.5 %collective-permute-start.6 = (f32[1024,256]{1,0:T(8,128)S(1)}, f32[1024,256]{1,0:T(8,128)S(1)}, u32[]{:S(2)}, u32[]{:S(2)}) collective-permute-start(f32[1024,256]{1,0:T(8,128)S(1)} %constant_dynamic-slice_fusion.1), channel_id=1, source_target_pairs={{0,16},{16,0},{1,17},{17,1},{2,18},{18,2},{3,19},{19,3},{4,20},{20... | collective-permute-start | bytes 3145736 | tf_op jit(solution)/shard_map/ppermute | solution.py:773
  20.6 18.3 %all-to-all-start = ((f32[16,1,2048]{2,1,0:T(1,128)}), f32[16,1,2048]{2,1,0:T(1,128)S(1)}, u32[]{:S(2)}, u32[]{:S(2)}) async-start(f32[16,1,2048]{2,1,0:T(1,128)} %all_to_all.22), calls=%async_computation | async-start | bytes 262144 | tf_op jit(solution)/shard_map/all_to_all | solution.py:602
  39.0 11.1 %collective-permute-start.4 = (f32[128,128]{1,0:T(8,128)S(1)}, f32[128,128]{1,0:T(8,128)S(1)}, u32[]{:S(2)}, u32[]{:S(2)}) collective-permute-start(f32[128,128]{1,0:T(8,128)S(1)} %reshape.97.refs_8_.refs_11_.refs_12_), channel_id=1, source_target_pairs={{0,16},{16,0},{1,17},{17,1},{2,18},{18,2},{3,19},{19,3},{4,20},{20... | collective-permute-start | bytes 196616 | tf_op jit(solution)/shard_map/ppermute | solution.py:773
  39.5 10.6 %collective-permute-start.2 = (f32[32,512]{1,0:T(8,128)S(1)}, f32[32,512]{1,0:T(8,128)S(1)}, u32[]{:S(2)}, u32[]{:S(2)}) collective-permute-start(f32[32,512]{1,0:T(8,128)S(1)} %reshape.96.refs_7_), channel_id=1, source_target_pairs={{0,16},{16,0},{1,17},{17,1},{2,18},{18,2},{3,19},{19,3},{4,20},{20... | collective-permute-start | bytes 196616 | tf_op jit(solution)/shard_map/ppermute | solution.py:773
  95.3 22.2 %collective-permute-start.9 = (f32[192,512]{1,0:T(8,128)}, f32[192,512]{1,0:T(8,128)S(1)}, u32[]{:S(2)}, u32[]{:S(2)}) collective-permute-start(f32[192,512]{1,0:T(8,128)} %get-tuple-element.111.refs_14_), channel_id=1, source_target_pairs={{0,1},{1,0},{2,3},{3,2},{4,5},{5,4},{6,7},{7,6},{8,9},{9,8},{10,11... | collective-permute-start | bytes 1179656 | tf_op jit(solution)/shard_map/ppermute | solution.py:678
  97.4 20.2 %collective-permute-start.10 = (f32[192,512]{1,0:T(8,128)}, f32[192,512]{1,0:T(8,128)S(1)}, u32[]{:S(2)}, u32[]{:S(2)}) collective-permute-start(f32[192,512]{1,0:T(8,128)} %get-tuple-element.112.refs_15_), channel_id=1, source_target_pairs={{0,2},{1,3},{2,0},{3,1},{4,6},{5,7},{6,4},{7,5},{8,10},{9,11},{10,... | collective-permute-start | bytes 1179656 | tf_op jit(solution)/shard_map/ppermute | solution.py:678
  98.8 18.8 %collective-permute-start.11 = (f32[192,512]{1,0:T(8,128)}, f32[192,512]{1,0:T(8,128)S(1)}, u32[]{:S(2)}, u32[]{:S(2)}) collective-permute-start(f32[192,512]{1,0:T(8,128)} %get-tuple-element.113.refs_16_), channel_id=1, source_target_pairs={{0,3},{1,2},{2,1},{3,0},{4,7},{5,6},{6,5},{7,4},{8,11},{9,10},{10,... | collective-permute-start | bytes 1179656 | tf_op jit(solution)/shard_map/ppermute | solution.py:678
  121.7 18.0 %collective-permute-start.15 = (f32[640,512]{1,0:T(8,128)}, f32[640,512]{1,0:T(8,128)S(1)}, u32[]{:S(2)}, u32[]{:S(2)}) collective-permute-start(f32[640,512]{1,0:T(8,128)} %get-tuple-element.128), channel_id=1, source_target_pairs={{0,16},{16,0},{1,17},{17,1},{2,18},{18,2},{3,19},{19,3},{4,20},{20... | collective-permute-start | bytes 3932168 | tf_op jit(solution)/shard_map/ppermute | solution.py:773
  122.2 17.4 %collective-permute-start.16 = (f32[192,128]{1,0:T(8,128)}, f32[192,128]{1,0:T(8,128)S(1)}, u32[]{:S(2)}, u32[]{:S(2)}) collective-permute-start(f32[192,128]{1,0:T(8,128)} %get-tuple-element.130), channel_id=1, source_target_pairs={{0,16},{16,0},{1,17},{17,1},{2,18},{18,2},{3,19},{19,3},{4,20},{20... | collective-permute-start | bytes 294920 | tf_op jit(solution)/shard_map/ppermute | solution.py:773
  122.2 17.4 %collective-permute-start.12 = (f32[48,512]{1,0:T(8,128)}, f32[48,512]{1,0:T(8,128)S(1)}, u32[]{:S(2)}, u32[]{:S(2)}) collective-permute-start(f32[48,512]{1,0:T(8,128)} %get-tuple-element.124.refs_7_), channel_id=1, source_target_pairs={{0,4},{1,5},{2,6},{3,7},{4,0},{5,1},{6,2},{7,3},{8,12},{9,13},{10,... | collective-permute-start | bytes 294920 | tf_op jit(solution)/shard_map/ppermute | solution.py:678
  124.2 15.4 %collective-permute-start.13 = (f32[48,512]{1,0:T(8,128)}, f32[48,512]{1,0:T(8,128)S(1)}, u32[]{:S(2)}, u32[]{:S(2)}) collective-permute-start(f32[48,512]{1,0:T(8,128)} %get-tuple-element.125.refs_8_), channel_id=1, source_target_pairs={{0,8},{1,9},{2,10},{3,11},{4,12},{5,13},{6,14},{7,15},{8,0},{9,1},... | collective-permute-start | bytes 294920 | tf_op jit(solution)/shard_map/ppermute | solution.py:678
  126.6 13.0 %collective-permute-start.14 = (f32[48,512]{1,0:T(8,128)}, f32[48,512]{1,0:T(8,128)S(1)}, u32[]{:S(2)}, u32[]{:S(2)}) collective-permute-start(f32[48,512]{1,0:T(8,128)} %get-tuple-element.126.refs_9_), channel_id=1, source_target_pairs={{0,12},{1,13},{2,14},{3,15},{4,8},{5,9},{6,10},{7,11},{8,4},{9,5},... | collective-permute-start | bytes 294920 | tf_op jit(solution)/shard_map/ppermute | solution.py:678
  143.8 25.8 %collective-permute-start.20 = (f32[48,512]{1,0:T(8,128)}, f32[48,512]{1,0:T(8,128)S(1)}, u32[]{:S(2)}, u32[]{:S(2)}) collective-permute-start(f32[48,512]{1,0:T(8,128)} %get-tuple-element.136.refs_7_.refs_0_), channel_id=1, source_target_pairs={{0,12},{1,13},{2,14},{3,15},{4,8},{5,9},{6,10},{7,11},{8,4},{9,5},... | collective-permute-start | bytes 294920 | tf_op jit(solution)/shard_map/ppermute | solution.py:630
  145.5 27.1 %collective-permute-start.19 = (f32[48,512]{1,0:T(8,128)}, f32[48,512]{1,0:T(8,128)S(1)}, u32[]{:S(2)}, u32[]{:S(2)}) collective-permute-start(f32[48,512]{1,0:T(8,128)} %get-tuple-element.136.refs_7_.refs_0_), channel_id=1, source_target_pairs={{0,8},{1,9},{2,10},{3,11},{4,12},{5,13},{6,14},{7,15},{8,0},{9,1},... | collective-permute-start | bytes 294920 | tf_op jit(solution)/shard_map/ppermute | solution.py:630
  148.4 21.1 %all-to-all-start.1 = ((f32[16,1,2048]{2,1,0:T(1,128)}), f32[16,1,2048]{2,1,0:T(1,128)S(1)}, u32[]{:S(2)}, u32[]{:S(2)}) async-start(f32[16,1,2048]{2,1,0:T(1,128)} %copy.62), calls=%async_computation.1 | async-start | bytes 262144 | tf_op jit(solution)/shard_map/all_to_all | solution.py:602
  154.8 19.6 %collective-permute-start.21 = (f32[160,512]{1,0:T(8,128)S(1)}, f32[160,512]{1,0:T(8,128)S(1)}, u32[]{:S(2)}, u32[]{:S(2)}) collective-permute-start(f32[160,512]{1,0:T(8,128)S(1)} %copy-done.63), channel_id=1, source_target_pairs={{0,1},{1,0},{2,3},{3,2},{4,5},{5,4},{6,7},{7,6},{8,9},{9,8},{10,11... | collective-permute-start | bytes 983048 | tf_op jit(solution)/shard_map/ppermute | solution.py:678
  156.8 17.5 %collective-permute-start.22 = (f32[160,512]{1,0:T(8,128)S(1)}, f32[160,512]{1,0:T(8,128)S(1)}, u32[]{:S(2)}, u32[]{:S(2)}) collective-permute-start(f32[160,512]{1,0:T(8,128)S(1)} %copy-done.62), channel_id=1, source_target_pairs={{0,2},{1,3},{2,0},{3,1},{4,6},{5,7},{6,4},{7,5},{8,10},{9,11},{10,... | collective-permute-start | bytes 983048 | tf_op jit(solution)/shard_map/ppermute | solution.py:678
  158.3 16.1 %collective-permute-start.23 = (f32[160,512]{1,0:T(8,128)S(1)}, f32[160,512]{1,0:T(8,128)S(1)}, u32[]{:S(2)}, u32[]{:S(2)}) collective-permute-start(f32[160,512]{1,0:T(8,128)S(1)} %copy-done.61), channel_id=1, source_target_pairs={{0,3},{1,2},{2,1},{3,0},{4,7},{5,6},{6,5},{7,4},{8,11},{9,10},{10,... | collective-permute-start | bytes 983048 | tf_op jit(solution)/shard_map/ppermute | solution.py:678
  183.9 21.1 %collective-permute-start.24 = (f32[96,1024]{1,0:T(8,128)}, f32[96,1024]{1,0:T(8,128)S(1)}, u32[]{:S(2)}, u32[]{:S(2)}) collective-permute-start(f32[96,1024]{1,0:T(8,128)} %get-tuple-element.147), channel_id=1, source_target_pairs={{0,16},{16,0},{1,17},{17,1},{2,18},{18,2},{3,19},{19,3},{4,20},{20... | collective-permute-start | bytes 1179656 | tf_op jit(solution)/shard_map/ppermute | solution.py:773
  200.3 17.6 %collective-permute-start.34 = (f32[192,512]{1,0:T(8,128)S(1)}, f32[192,512]{1,0:T(8,128)S(1)}, u32[]{:S(2)}, u32[]{:S(2)}) collective-permute-start(f32[192,512]{1,0:T(8,128)S(1)} %copy-done.22), channel_id=1, source_target_pairs={{0,3},{1,2},{2,1},{3,0},{4,7},{5,6},{6,5},{7,4},{8,11},{9,10},{10,... | collective-permute-start | bytes 1179656 | tf_op jit(solution)/shard_map/ppermute | solution.py:630
  202.7 15.4 %collective-permute-start.33 = (f32[192,512]{1,0:T(8,128)S(1)}, f32[192,512]{1,0:T(8,128)S(1)}, u32[]{:S(2)}, u32[]{:S(2)}) collective-permute-start(f32[192,512]{1,0:T(8,128)S(1)} %copy-done.22), channel_id=1, source_target_pairs={{0,2},{1,3},{2,0},{3,1},{4,6},{5,7},{6,4},{7,5},{8,10},{9,11},{10,... | collective-permute-start | bytes 1179656 | tf_op jit(solution)/shard_map/ppermute | solution.py:630
  203.2 14.9 %collective-permute-start.32 = (f32[192,512]{1,0:T(8,128)S(1)}, f32[192,512]{1,0:T(8,128)S(1)}, u32[]{:S(2)}, u32[]{:S(2)}) collective-permute-start(f32[192,512]{1,0:T(8,128)S(1)} %copy-done.22), channel_id=1, source_target_pairs={{0,1},{1,0},{2,3},{3,2},{4,5},{5,4},{6,7},{7,6},{8,9},{9,8},{10,11... | collective-permute-start | bytes 1179656 | tf_op jit(solution)/shard_map/ppermute | solution.py:630
  204.4 13.5 %collective-permute-start.30 = (f32[40,512]{1,0:T(8,128)}, f32[40,512]{1,0:T(8,128)S(1)}, u32[]{:S(2)}, u32[]{:S(2)}) collective-permute-start(f32[40,512]{1,0:T(8,128)} %phase_quad.1.refs_12_.refs_0_), channel_id=1, source_target_pairs={{0,8},{1,9},{2,10},{3,11},{4,12},{5,13},{6,14},{7,15},{8,0},{9,1},... | collective-permute-start | bytes 245768 | tf_op jit(solution)/shard_map/ppermute | solution.py:630
  205.0 12.9 %collective-permute-start.29 = (f32[40,512]{1,0:T(8,128)}, f32[40,512]{1,0:T(8,128)S(1)}, u32[]{:S(2)}, u32[]{:S(2)}) collective-permute-start(f32[40,512]{1,0:T(8,128)} %phase_quad.1.refs_12_.refs_0_), channel_id=1, source_target_pairs={{0,4},{1,5},{2,6},{3,7},{4,0},{5,1},{6,2},{7,3},{8,12},{9,13},{10,... | collective-permute-start | bytes 245768 | tf_op jit(solution)/shard_map/ppermute | solution.py:630
  226.1 29.6 %all-to-all-start.2 = ((f32[16,16,512]{2,1,0:T(8,128)}), f32[16,16,512]{2,1,0:T(8,128)S(1)}, u32[]{:S(2)}, u32[]{:S(2)}) async-start(f32[16,16,512]{2,1,0:T(8,128)} %bitcast.37), calls=%async_computation.2 | async-start | bytes 1048576 | tf_op jit(solution)/shard_map/all_to_all | solution.py:602
  232.4 33.7 %collective-permute-start.5 = (f32[1024,256]{1,0:T(8,128)}, f32[1024,256]{1,0:T(8,128)}, u32[]{:S(2)}, u32[]{:S(2)}) collective-permute-start(f32[1024,256]{1,0:T(8,128)} %get-tuple-element.100), channel_id=1, source_target_pairs={{0,16},{16,0},{1,17},{17,1},{2,18},{18,2},{3,19},{19,3},{4,20},{20... | collective-permute-start | bytes 3145736 | tf_op jit(solution)/shard_map/ppermute | solution.py:773
  233.1 15.8 %collective-permute-start.42 = (f32[160,512]{1,0:T(8,128)}, f32[160,512]{1,0:T(8,128)S(1)}, u32[]{:S(2)}, u32[]{:S(2)}) collective-permute-start(f32[160,512]{1,0:T(8,128)} %get-tuple-element.155.refs_2_.refs_1_), channel_id=1, source_target_pairs={{0,3},{1,2},{2,1},{3,0},{4,7},{5,6},{6,5},{7,4},{8,11},{9,10},{10,... | collective-permute-start | bytes 983048 | tf_op jit(solution)/shard_map/ppermute | solution.py:630
  236.0 18.3 %collective-permute-start.41 = (f32[160,512]{1,0:T(8,128)}, f32[160,512]{1,0:T(8,128)S(1)}, u32[]{:S(2)}, u32[]{:S(2)}) collective-permute-start(f32[160,512]{1,0:T(8,128)} %get-tuple-element.155.refs_2_.refs_1_), channel_id=1, source_target_pairs={{0,2},{1,3},{2,0},{3,1},{4,6},{5,7},{6,4},{7,5},{8,10},{9,11},{10,... | collective-permute-start | bytes 983048 | tf_op jit(solution)/shard_map/ppermute | solution.py:630
  236.6 19.1 %collective-permute-start.40 = (f32[160,512]{1,0:T(8,128)}, f32[160,512]{1,0:T(8,128)}, u32[]{:S(2)}, u32[]{:S(2)}) collective-permute-start(f32[160,512]{1,0:T(8,128)} %get-tuple-element.155.refs_2_.refs_1_), channel_id=1, source_target_pairs={{0,1},{1,0},{2,3},{3,2},{4,5},{5,4},{6,7},{7,6},{8,9},{9,8},{10,11... | collective-permute-start | bytes 983048 | tf_op jit(solution)/shard_map/ppermute | solution.py:630
  237.2 32.8 %collective-permute-start.28 = (f32[1024,256]{1,0:T(8,128)}, f32[1024,256]{1,0:T(8,128)}, u32[]{:S(2)}, u32[]{:S(2)}) collective-permute-start(f32[1024,256]{1,0:T(8,128)} %get-tuple-element.150), channel_id=1, source_target_pairs={{0,16},{16,0},{1,17},{17,1},{2,18},{18,2},{3,19},{19,3},{4,20},{20... | collective-permute-start | bytes 3145736 | tf_op jit(solution)/shard_map/ppermute | solution.py:773
  259.8 20.5 %all-to-all-start.3 = ((f32[16,16,512]{2,1,0:T(8,128)}), f32[16,16,512]{2,1,0:T(8,128)S(1)}, u32[]{:S(2)}, u32[]{:S(2)}) async-start(f32[16,16,512]{2,1,0:T(8,128)} %broadcast_in_dim.16), calls=%async_computation.3 | async-start | bytes 1048576 | tf_op jit(solution)/shard_map/all_to_all | solution.py:602
  (91 other events, 417.0 us)
